TPU v7x, 256 devices: a whole 4x4x8 slice. The times are simulated.
256 devices in a mesh: seq: 64 (over z_hi, x, y, core), head: 4 (over z_lo).
Axes of the slice: x: 4, y: 4, z: 8 (z_hi: 2, z_lo: 4; z = z_hi * 4 + z_lo), core: 2. Of those that a mesh axis runs over, the one named last changes fastest.
Arguments:
- video_query: bfloat16 [32768, 3072], P('seq', 'head'), may hold values from -18 to 18
- video_key: bfloat16 [32768, 3072], P('seq', 'head'), may hold values from -18 to 18
- video_value: bfloat16 [32768, 3072], P('seq', 'head'), may hold values from -6 to 6
- video_grad_out: bfloat16 [32768, 3072], P('seq', 'head'), may hold values from -6 to 6
- audio_query: bfloat16 [512, 3072], P('seq', 'head'), may hold values from -18 to 18
- audio_key: bfloat16 [512, 3072], P('seq', 'head'), may hold values from -18 to 18
- audio_value: bfloat16 [512, 3072], P('seq', 'head'), may hold values from -6 to 6
- audio_grad_out: bfloat16 [512, 3072], P('seq', 'head'), may hold values from -6 to 6
- video_query_gain: float32 [3072], P('head'), may hold values from 0.25 to 1.75
- video_key_gain: float32 [3072], P('head'), may hold values from 0.25 to 1.75
- audio_query_gain: float32 [3072], P('head'), may hold values from 0.25 to 1.75
- audio_key_gain: float32 [3072], P('head'), may hold values from 0.25 to 1.75
Outputs:
- video_out: bfloat16 [32768, 3072], P('seq', 'head')
- audio_out: bfloat16 [512, 3072], P('seq', 'head')
- grad_video_query: bfloat16 [32768, 3072], P('seq', 'head')
- grad_video_key: bfloat16 [32768, 3072], P('seq', 'head')
- grad_video_value: bfloat16 [32768, 3072], P('seq', 'head')
- grad_audio_query: bfloat16 [512, 3072], P('seq', 'head')
- grad_audio_key: bfloat16 [512, 3072], P('seq', 'head')
- grad_audio_value: bfloat16 [512, 3072], P('seq', 'head')
All inputs are finite; a program needn't handle non-finite values.
Results may differ from a plain program's by a relative error of at most 0.034.
Values may be sent and summed in bfloat16 or wider, within the bound.
A program may use at most 128 MiB of HBM per device.

v0:
```python
import math

import jax
import jax.numpy as jnp
from jax import lax
from jax.sharding import PartitionSpec as P

HEADS = 24
HEAD_DIM = 128


EPS = 1e-06


def split_heads(array, heads):
    return array.reshape(array.shape[0], heads, array.shape[1] // heads)


def square_sum(raw):
    values = raw.astype(jnp.float32)
    return jnp.sum(values * values, axis=1)


def grad_inner(raw, gain, grad):
    return jnp.sum(raw.astype(jnp.float32) * gain * grad, axis=1)


def shards(
    video_query,
    video_key,
    video_value,
    video_grad_out,
    audio_query,
    audio_key,
    audio_value,
    audio_grad_out,
    video_query_gain,
    video_key_gain,
    audio_query_gain,
    audio_key_gain,
):
    width = HEADS * HEAD_DIM
    heads = video_query.shape[1] // HEAD_DIM
    factor = 1.0 / math.sqrt(HEAD_DIM)
    video_rows = video_query.shape[0]
    own = audio_query.shape[0]
    raws = (video_query, video_key, audio_query, audio_key)
    gains = (video_query_gain, video_key_gain, audio_query_gain, audio_key_gain)
    sums = lax.psum(
        (
            square_sum(video_query),
            square_sum(video_key),
            square_sum(audio_query),
            square_sum(audio_key),
        ),
        "head",
    )
    inverses = [lax.rsqrt(total[:, None] / width + EPS) for total in sums]
    normed = [
        (raw.astype(jnp.float32) * inv_row * gain).astype(jnp.bfloat16)
        for raw, inv_row, gain in zip(raws, inverses, gains)
    ]
    keys_all, values_all, queries_all, cotan_all = (
        lax.all_gather(normed[3], "seq", axis=0, tiled=True),
        lax.all_gather(audio_value, "seq", axis=0, tiled=True),
        lax.all_gather(normed[2], "seq", axis=0, tiled=True),
        lax.all_gather(audio_grad_out, "seq", axis=0, tiled=True),
    )
    vq3 = split_heads(normed[0], heads)
    vdo3 = split_heads(video_grad_out, heads)
    key3 = split_heads(keys_all, heads)
    val3 = split_heads(values_all, heads)
    scores = jnp.einsum("rhd,khd->hrk", vq3, key3, preferred_element_type=jnp.float32) * factor
    expo = jnp.exp(scores - jnp.max(scores, axis=2, keepdims=True))
    probs = expo / jnp.sum(expo, axis=2, keepdims=True)
    probs_low = probs.astype(jnp.bfloat16)
    video_out3 = jnp.einsum(
        "hrk,khd->rhd", probs_low, val3, preferred_element_type=jnp.float32
    ).astype(jnp.bfloat16)
    row_dot = jnp.sum(vdo3.astype(jnp.float32) * video_out3.astype(jnp.float32), axis=2)
    dprob = jnp.einsum("rhd,khd->hrk", vdo3, val3, preferred_element_type=jnp.float32)
    dscore = (probs * (dprob - row_dot.T[:, :, None])).astype(jnp.bfloat16)
    grad_vqn = (
        jnp.einsum("hrk,khd->rhd", dscore, key3, preferred_element_type=jnp.float32) * factor
    ).reshape(video_rows, -1)
    ds_part = dscore
    grad_k = jnp.einsum("hrk,rhd->khd", ds_part, vq3, preferred_element_type=jnp.float32) * factor
    grad_v = jnp.einsum("hrk,rhd->khd", probs_low, vdo3, preferred_element_type=jnp.float32)
    key_part = lax.psum_scatter(
        jnp.concatenate(
            (
                grad_k.reshape(own * lax.axis_size("seq"), -1),
                grad_v.reshape(own * lax.axis_size("seq"), -1),
            ),
            axis=1,
        ),
        "seq",
        scatter_dimension=0,
        tiled=True,
    )
    qa3 = split_heads(queries_all, heads)
    doa3 = split_heads(cotan_all, heads)
    vk3 = split_heads(normed[1], heads)
    vv3 = split_heads(video_value, heads)
    scores_a = jnp.einsum("qhd,khd->hqk", qa3, vk3, preferred_element_type=jnp.float32) * factor
    top_all = lax.pmax(jnp.max(scores_a, axis=2), "seq")
    expo_a = jnp.exp(scores_a - top_all[:, :, None])
    total_local = jnp.sum(expo_a, axis=2).T
    numer_local = jnp.einsum(
        "hqk,khd->qhd", expo_a.astype(jnp.bfloat16), vv3, preferred_element_type=jnp.float32
    ).reshape(queries_all.shape[0], -1)
    first = lax.axis_index("seq") * own
    numer, total = (
        lax.psum_scatter(numer_local, "seq", scatter_dimension=0, tiled=True),
        lax.psum_scatter(total_local, "seq", scatter_dimension=0, tiled=True),
    )
    audio_out3 = (split_heads(numer, heads) / total[:, :, None]).astype(jnp.bfloat16)
    own_top = lax.dynamic_slice_in_dim(top_all, first, own, 1).T
    own_dot = jnp.sum(
        split_heads(audio_grad_out, heads).astype(jnp.float32) * audio_out3.astype(jnp.float32),
        axis=2,
    )
    log_total, row_dot_a = (
        lax.all_gather(own_top + jnp.log(total), "seq", axis=0, tiled=True),
        lax.all_gather(own_dot, "seq", axis=0, tiled=True),
    )
    feat = heads * HEAD_DIM
    grad_akn = key_part[:, :feat]
    grad_audio_value = key_part[:, feat:].astype(jnp.bfloat16)
    audio_out = audio_out3.reshape(own, -1)
    probs_a = jnp.exp(scores_a - log_total.T[:, :, None])
    probs_a_low = probs_a.astype(jnp.bfloat16)
    grad_video_value = (
        jnp.einsum("hqk,qhd->khd", probs_a_low, doa3, preferred_element_type=jnp.float32)
        .astype(jnp.bfloat16)
        .reshape(video_rows, -1)
    )
    dprob_a = jnp.einsum("qhd,khd->hqk", doa3, vv3, preferred_element_type=jnp.float32)
    dscore_a = (probs_a * (dprob_a - row_dot_a.T[:, :, None])).astype(jnp.bfloat16)
    grad_vkn = (
        jnp.einsum("hqk,qhd->khd", dscore_a, qa3, preferred_element_type=jnp.float32) * factor
    ).reshape(video_rows, -1)
    ds_part = dscore_a
    grad_aqn = lax.psum_scatter(
        (
            jnp.einsum("hqk,khd->qhd", ds_part, vk3, preferred_element_type=jnp.float32) * factor
        ).reshape(own * lax.axis_size("seq"), -1),
        "seq",
        scatter_dimension=0,
        tiled=True,
    )
    grads = (grad_vqn, grad_vkn, grad_aqn, grad_akn)
    inners = lax.psum(
        (
            grad_inner(video_query, video_query_gain, grad_vqn),
            grad_inner(video_key, video_key_gain, grad_vkn),
            grad_inner(audio_query, audio_query_gain, grad_aqn),
            grad_inner(audio_key, audio_key_gain, grad_akn),
        ),
        "head",
    )
    finals = []
    for raw, inv_row, gain, grad, inner in zip(raws, inverses, gains, grads, inners):
        cube = inv_row * inv_row * inv_row
        finals.append(
            (
                inv_row * gain * grad - raw.astype(jnp.float32) * cube * inner[:, None] / width
            ).astype(jnp.bfloat16)
        )
    video_out = video_out3.reshape(video_rows, -1)
    return (
        video_out,
        audio_out,
        finals[0],
        finals[1],
        grad_video_value,
        finals[2],
        finals[3],
        grad_audio_value,
    )


def solution(mesh):
    placed = (
        P("seq", "head"),
        P("seq", "head"),
        P("seq", "head"),
        P("seq", "head"),
        P("seq", "head"),
        P("seq", "head"),
        P("seq", "head"),
        P("seq", "head"),
        P("head"),
        P("head"),
        P("head"),
        P("head"),
    )
    return jax.shard_map(
        shards,
        mesh=mesh,
        in_specs=placed,
        out_specs=(
            P("seq", "head"),
            P("seq", "head"),
            P("seq", "head"),
            P("seq", "head"),
            P("seq", "head"),
            P("seq", "head"),
            P("seq", "head"),
            P("seq", "head"),
        ),
        check_vma=False,
    )
```

profile of v0, /device:TPU:1, one launch (start us, length us, event | category | flops | bytes accessed | tf_op | source)
XLA Modules:
  0.0 1736.6 jit_solution(14767706803768685730)
XLA Ops:
  10.9 11.9 all-reduce.2
  22.9 121.3 %all_gather.20 = bf16[512,768]{1,0:T(8,128)(2,1)S(1)} all-gather(bf16[8,768]{1,0:T(8,128)(2,1)S(1)} %fusion.51), channel_id=1, replica_groups=mesh['seq'=64,'head'=4] {'seq'}, dimensions={0}, use_global_device_ids=true | all-gather | bytes 798720 | tf_op jit(solution)/shard_map/all_gather | solution.py:66
  146.5 3.7 multiply_reduce_fusion.1
  150.2 389.9 %pmax.7 = f32[6,512]{1,0:T(8,128)S(1)} all-reduce(f32[6,512]{1,0:T(8,128)S(1)} %get-tuple-element.60), channel_id=1, replica_groups=mesh['seq'=64,'head'=4] {'seq'}, use_global_device_ids=true, to_apply=%region_11.0 | all-reduce | flops 3072 | bytes 24576 | tf_op jit(solution)/shard_map/pmax | solution.py:106
  540.1 5.2 fusion.9
  545.4 3.1 copy.137
  548.7 119.9 %all_gather.18 = bf16[512,768]{1,0:T(8,128)(2,1)S(1)} all-gather(bf16[8,768]{1,0:T(8,128)(2,1)S(1)} %fusion.42), channel_id=1, replica_groups=mesh['seq'=64,'head'=4] {'seq'}, dimensions={0}, use_global_device_ids=true | all-gather | bytes 798720 | tf_op jit(solution)/shard_map/all_gather | solution.py:64
  670.0 116.8 %all_gather.19 = bf16[512,768]{1,0:T(8,128)(2,1)} all-gather(bf16[8,768]{1,0:T(8,128)(2,1)S(1)} %copy-done.33), channel_id=1, replica_groups=mesh['seq'=64,'head'=4] {'seq'}, dimensions={0}, use_global_device_ids=true | all-gather | bytes 798720 | tf_op jit(solution)/shard_map/all_gather | solution.py:65
  787.1 4.8 fusion.64
  791.9 3.7 fusion.16
  800.3 3.0 multiply_reduce_fusion.2
  803.3 4.0 multiply_convert_fusion.1
  813.3 111.4 %all_gather.22 = bf16[512,768]{1,0:T(8,128)(2,1)S(1)} all-gather(bf16[8,768]{1,0:T(8,128)(2,1)S(1)} %copy-done.28), channel_id=1, replica_groups=mesh['seq'=64,'head'=4] {'seq'}, dimensions={0}, use_global_device_ids=true | all-gather | bytes 798720 | tf_op jit(solution)/shard_map/all_gather | solution.py:67
  927.1 3.9 fusion.1
  931.0 390.4 %all-reduce = f32[512,6]{0,1:T(8,128)S(1)} all-reduce(f32[512,6]{0,1:T(8,128)S(1)} %bitcast.114), channel_id=3, replica_groups=mesh['seq'=64,'head'=4] {'seq'}, use_global_device_ids=true, to_apply=%region_14.0.clone | all-reduce | flops 3072 | bytes 24576
  1321.5 118.4 %all_gather.21 = f32[512,6]{1,0:T(8,128)S(1)} all-gather(f32[8,6]{1,0:T(8,128)S(1)} %copy.143), channel_id=1, replica_groups=mesh['seq'=64,'head'=4] {'seq'}, dimensions={0}, use_global_device_ids=true | all-gather | bytes 12480 | tf_op jit(solution)/shard_map/all_gather | solution.py:124
  1441.0 110.2 %all_gather.23 = f32[512,6]{1,0:T(8,128)S(1)} all-gather(f32[8,6]{1,0:T(8,128)S(1)} %copy.148), channel_id=1, replica_groups=mesh['seq'=64,'head'=4] {'seq'}, dimensions={0}, use_global_device_ids=true | all-gather | bytes 12480 | tf_op jit(solution)/shard_map/all_gather | solution.py:125
  1551.4 5.2 multiply_convert_fusion
  1558.3 3.1 copy.184
  1563.7 5.1 fusion.35
  1571.1 2.9 convolution_multiply_fusion.3
  1581.1 132.9 %reduce-scatter.11.cloned.1.call-done = f32[8,768]{1,0:T(8,128)} async-done(((f32[512,768]{1,0:T(8,128)}), f32[8,768]{1,0:T(8,128)}) %reduce-scatter.11.cloned.1.call-update) | async-done | bytes 24592 | tf_op jit(solution)/shard_map/reduce_scatter | solution.py:144
  1714.8 7.3 all-reduce.1
  1722.2 2.7 fusion.23
  (124 shorter events, 40.9 us)
Async XLA Ops:
  7.2 15.7 copy-start.32
  7.2 1432.8 %reduce-scatter.9.cloned.1.call-start = ((), (), s32[]{:S(2)}) async-start(), calls=%async_computation.3 | async-start | bytes 1597440 | tf_op jit(solution)/shard_map/reduce_scatter | solution.py:114
  8.7 778.2 %copy-start.3 = (bf16[512,768]{0,1:T(8,128)(2,1)}, bf16[512,768]{0,1:T(8,128)(2,1)S(1)}, u32[]{:S(2)}) copy-start(bf16[512,768]{0,1:T(8,128)(2,1)S(1)} %copy.125) | copy-start | bytes 2359300
  10.4 136.1 %copy-start = (bf16[512,768]{0,1:T(8,128)(2,1)}, bf16[512,768]{0,1:T(8,128)(2,1)S(1)}, u32[]{:S(2)}) copy-start(bf16[512,768]{0,1:T(8,128)(2,1)S(1)} %copy.132) | copy-start | bytes 2359300
  10.4 135.8 %copy-start.30 = (f32[768]{0:T(1024)S(1)}, f32[768]{0:T(1024)}, u32[]{:S(2)}) copy-start(f32[768]{0:T(1024)} %param.21) | copy-start | bytes 9220
  144.5 5.7 copy-start.13
  146.2 393.9 %copy-start.10 = (bf16[512,768]{0,1:T(8,128)(2,1)}, bf16[512,768]{0,1:T(8,128)(2,1)S(1)}, u32[]{:S(2)}) copy-start(bf16[512,768]{0,1:T(8,128)(2,1)S(1)} %copy.135) | copy-start | bytes 2359300
  545.4 123.5 %copy-start.22 = (bf16[512,768]{1,0:T(8,128)(2,1)S(1)}, bf16[512,768]{1,0:T(8,128)(2,1)}, u32[]{:S(2)}) copy-start(bf16[512,768]{1,0:T(8,128)(2,1)} %param.15) | copy-start | bytes 2359300
  548.5 121.5 %copy-start.33 = (bf16[8,768]{1,0:T(8,128)(2,1)S(1)}, bf16[8,768]{1,0:T(8,128)(2,1)}, u32[]{:S(2)}) copy-start(bf16[8,768]{1,0:T(8,128)(2,1)} %param.18) | copy-start | bytes 36868
  548.5 238.4 %copy-start.29 = (f32[768]{0:T(1024)S(1)}, f32[768]{0:T(1024)}, u32[]{:S(2)}) copy-start(f32[768]{0:T(1024)} %param.20) | copy-start | bytes 9220
  548.6 1029.9 %reduce-scatter.13.cloned.1.call-start = ((), (), s32[]{:S(2)}) async-start(), calls=%async_computation.5 | async-start | bytes 3194880 | tf_op jit(solution)/shard_map/reduce_scatter | solution.py:89
  668.9 123.1 %copy-start.18 = (bf16[512,768]{0,1:T(8,128)(2,1)}, bf16[512,768]{0,1:T(8,128)(2,1)S(1)}, u32[]{:S(2)}) copy-start(bf16[512,768]{0,1:T(8,128)(2,1)S(1)} %copy.126) | copy-start | bytes 2359300
  787.1 4.8 copy-start.19
  803.2 4.0 copy-start.20
  812.5 113.3 %copy-start.34 = (u32[256]{0:T(256)S(1)}, u32[256]{0:T(256)}, u32[]{:S(2)}) copy-start(u32[256]{0:T(256)} %constant.41) | copy-start | bytes 3076
  812.6 901.4 %reduce-scatter.11.cloned.1.call-start = ((), (), s32[]{:S(2)}) async-start(), calls=%async_computation.4 | async-start | bytes 1597440 | tf_op jit(solution)/shard_map/reduce_scatter | solution.py:144
  1551.4 5.2 copy-start.16
  1571.1 4.0 copy-start.4
  1571.1 4.3 copy-start.14
  1576.7 145.5 %copy-start.5 = (bf16[512,768]{0,1:T(8,128)(2,1)S(1)}, bf16[512,768]{0,1:T(8,128)(2,1)}, u32[]{:S(2)}) copy-start(bf16[512,768]{0,1:T(8,128)(2,1)} %copy-done.3) | copy-start | bytes 2359300
  1577.8 149.4 %copy-start.2 = (bf16[512,768]{0,1:T(8,128)(2,1)S(1)}, bf16[512,768]{0,1:T(8,128)(2,1)}, u32[]{:S(2)}) copy-start(bf16[512,768]{0,1:T(8,128)(2,1)} %copy-done) | copy-start | bytes 2359300
  1578.5 148.7 %copy-start.7 = (f32[6,128,512]{2,1,0:T(8,128)S(1)}, f32[6,128,512]{2,1,0:T(8,128)}, u32[]{:S(2)}) copy-start(f32[6,128,512]{2,1,0:T(8,128)} %copy-done.6) | copy-start | bytes 4718596
  1724.8 3.9 copy-start.27
  1724.9 4.5 copy-start.26
  (14 other events, 33.7 us)
Sparse Core Ops, SparseCore 0:
  548.7 159.7 reduce-scatter.8
  812.7 157.0 reduce-scatter.12
  1561.5 152.3 reduce-scatter.10
where the time goes:
time: 1740 us
  blocking collectives  1500 us (86%)
  waiting for transfers between devices  133 us (8%)
  matrix products  40.2 us (2%)
  local copies, waits for them, and re-layouts  33.5 us (2%)
  other arithmetic  17.5 us (1%)
    unnamed x1, blocking collectives  390 us
    pmax x1, blocking collectives, shards(): top_all = lax.pmax(jnp.max(scores_a, axis=2), 'seq')  390 us
    reduce_scatter x1, waiting for transfers between devices, shards(): lax.psum_scatter((jnp.einsum('hqk,khd->qhd', ds_part, vk3, preferred_elem...  133 us
    all_gather x1, blocking collectives, shards(): lax.all_gather(normed[2], 'seq', axis=0, tiled=True)  121 us
    all_gather x1, blocking collectives, shards(): lax.all_gather(normed[3], 'seq', axis=0, tiled=True)  120 us
    all_gather x1, blocking collectives, shards(): lax.all_gather(own_top + jnp.log(total), 'seq', axis=0, tiled=True)  118 us
    all_gather x1, blocking collectives, shards(): lax.all_gather(audio_value, 'seq', axis=0, tiled=True)  117 us
    all_gather x1, blocking collectives, shards(): lax.all_gather(audio_grad_out, 'seq', axis=0, tiled=True)  111 us
  transfers between devices with their start and end apart: 3, of which 1 were waited for; matrix products, arithmetic and copies ran while one was open for 3% of the time, Pallas kernels for 0%

commit v1 on v0

v1 whole, which is shorter than its diff:
```python
import math

import jax
import jax.numpy as jnp
from jax import lax
from jax.experimental import pallas as pl
from jax.experimental.pallas import tpu as pltpu
from jax.sharding import PartitionSpec as P

HEADS = 24
D = 128
WIDTH = HEADS * D
EPS = 1e-06
FACTOR = 1.0 / math.sqrt(D)
KLOG = FACTOR * math.log2(math.e)
ROWS = 512
TOK = 512
LOCAL = 768
HALF = 384
NH = 6
F32 = jnp.float32
BF16 = jnp.bfloat16
MESH = pl.DeviceIdType.MESH
NT = (((1,), (1,)), ((), ()))
TN = (((0,), (0,)), ((), ()))
NN = (((1,), (0,)), ((), ()))


def dot(a, b, dims):
    return lax.dot_general(a, b, dims, preferred_element_type=F32)


def col(row):
    return jnp.transpose(jnp.broadcast_to(row, (D, ROWS)))


def row_of(square):
    return jnp.sum(jnp.transpose(square), axis=0, keepdims=True)


def kernel(
    vq, vk, vv, vdo, aq, ak, av, ado, gvq_gain, gvk_gain, gaq_gain, gak_gain,
    video_out, out_gvq, out_gvk, out_gvv, out_small,
    G, CXs, CXr, HS, HI, HA, vqn, vkn, inv_col, E, DP, ST, SR, WT,
    GQ, GK, IA, Xs, Xr, R, RB1, RB2, S, RB3, TZ, RB4, FS, FR, sm,
    send, recv,
):
    s = lax.axis_index("seq")
    hd = lax.axis_index("head")
    c = s % 2
    y = (s // 2) % 4
    x = (s // 8) % 4
    zh = s // 32
    p = x + c * (y - x)
    q = y + c * (x - y)
    o = 1 - c

    def at(zz, pp, qq):
        xx = pp + c * (qq - pp)
        yy = qq + c * (pp - qq)
        return {"seq": ((zz * 4 + xx) * 4 + yy) * 2 + c}

    sib = {"seq": s + 1 - 2 * c}
    opp = at(1 - zh, p, q)
    opp_sib = {"seq": s + 1 - 2 * c + 32 - 64 * zh}
    ring_p = [at(zh, (p + k) % 4, q) for k in (1, 2, 3)]
    ring_q = [at(zh, p, (q + k) % 4) for k in (1, 2, 3)]
    heads = [{"head": (hd + k) % 4} for k in (1, 2, 3)]
    pn, pb = (p + 1) % 4, (p + 3) % 4
    qn, qb = (q + 1) % 4, (q + 3) % 4
    q2 = (q + 2) % 4
    right_p, left_p = ring_p[0], ring_p[2]
    right_q, left_q = ring_q[0], ring_q[2]

    barrier = pltpu.get_barrier_semaphore()
    partners = [sib, opp, opp_sib] + ring_p + ring_q + heads
    for partner in partners:
        pl.semaphore_signal(barrier, inc=1, device_id=partner, device_id_type=MESH)
    pl.semaphore_wait(barrier, len(partners))

    count = [0]

    def copy(src, dst, to, slot=None):
        if slot is None:
            slot = count[0]
            count[0] += 1
        made = pltpu.make_async_remote_copy(
            src_ref=src,
            dst_ref=dst,
            send_sem=send.at[slot],
            recv_sem=recv.at[slot],
            device_id=to,
            device_id_type=MESH,
        )
        return made

    def go(*copies):
        for one in copies:
            one.start()
        return copies

    def done(copies):
        for one in copies:
            one.wait()

    my_half = pl.ds(pl.multiple_of(c * HALF, D), HALF)
    its_half = pl.ds(pl.multiple_of(o * HALF, D), HALF)

    def ag_core(ch, refs):
        for a, ref in enumerate(refs):
            CXs[ch, a] = ref[:, its_half].astype(F32)
        return go(copy(CXs.at[ch], CXr.at[ch], sib))

    def ag_z(ch, refs):
        for a, ref in enumerate(refs):
            mine = ref[:, my_half].astype(F32)
            other = CXr[ch, a]
            low = jnp.where(c == 0, mine, other)
            high = jnp.where(c == 0, other, mine)
            G[c, ch, q, p, zh, a] = jnp.concatenate([low, high], axis=0).astype(BF16)
        block = G.at[c, ch, q, p, zh]
        return go(copy(block, block, opp))

    def ag_p1(ch):
        block = G.at[c, ch, q, p]
        return go(copy(block, block, right_p), copy(block, block, left_p))

    def ag_p2(ch):
        one, two = G.at[c, ch, q, pb, 0], G.at[c, ch, q, pn, 1]
        return go(copy(one, one, right_p), copy(two, two, left_p))

    def forward(ch, i):
        block = G.at[c, ch, i]
        return go(copy(block, block, sib))

    def ag_q1(ch):
        block = G.at[c, ch, q]
        return go(copy(block, block, right_q), copy(block, block, left_q))

    def ag_q2(ch):
        one, two = G.at[c, ch, qb, 0:2], G.at[c, ch, qn, 2:4]
        return go(copy(one, one, right_q), copy(two, two, left_q))

    core0 = ag_core(0, (av, ado))

    HS[hd] = jnp.zeros((16, 512), F32)
    for i, raw in enumerate((vq, vk)):
        total = jnp.zeros((ROWS, D), F32)
        for b in range(NH):
            block = raw[:, b * D : (b + 1) * D].astype(F32)
            total = total + block * block
        HS[hd, i : i + 1, :] = row_of(total)
    for i, raw in enumerate((aq, ak)):
        block = raw[...].astype(F32)
        total = jnp.sum(block * block, axis=1, keepdims=True)
        HS[hd, 8:16, i * D : (i + 1) * D] = jnp.broadcast_to(total, (8, D))
    sums = go(*[copy(HS.at[hd], HS.at[hd], to) for to in heads])

    done(core0)
    z0 = ag_z(0, (av, ado))
    done(sums)
    total = HS[0] + HS[1] + HS[2] + HS[3]
    inv = lax.rsqrt(total / WIDTH + EPS)
    inv_a = [inv[8:16, 0:D], inv[8:16, D : 2 * D]]
    for i, (raw, gain) in enumerate(((aq, gaq_gain), (ak, gak_gain))):
        wide = jnp.concatenate([inv_a[i]] * NH, axis=1)
        sm[i] = (raw[...].astype(F32) * wide * gain[...]).astype(BF16).astype(F32)
    normed_audio = (sm.at[0], sm.at[1])
    core1 = ag_core(1, normed_audio)
    done(z0)
    p10 = ag_p1(0)
    done(core1)
    z1 = ag_z(1, normed_audio)

    for i, (raw, gain, out) in enumerate(((vq, gvq_gain, vqn), (vk, gvk_gain, vkn))):
        inv_col[i] = col(inv[i : i + 1, :])
        for b in range(NH):
            at_b = slice(b * D, (b + 1) * D)
            out[:, at_b] = (raw[:, at_b].astype(F32) * inv_col[i] * gain[:, at_b]).astype(BF16)

    done(p10)
    p20 = ag_p2(0)
    done(z1)
    p11 = ag_p1(1)
    done(p20)
    q10 = ag_q1(0)
    f0 = forward(0, q)
    done(p11)
    p21 = ag_p2(1)
    done(p21)
    q11 = ag_q1(1)
    f1 = forward(1, q)
    done(q10)
    q20 = ag_q2(0)
    f0 += forward(0, qn) + forward(0, qb)
    done(q11)
    q21 = ag_q2(1)
    f1 += forward(1, qn) + forward(1, qb)
    done(q20)
    f0 += forward(0, q2)
    done(q21)
    f1 += forward(1, q2)

    def lanes_of(i):
        return pl.ds(pl.multiple_of(i * D, D), D)

    ST[...] = jnp.zeros_like(ST)

    def first_pass(h, j):
        head = 3 * h + j
        lanes, jl = lanes_of(head), lanes_of(j)
        for t in range(2):
            chunk = slice(256 * t, 256 * (t + 1))
            qs = G[h, 1, 2 * t : 2 * t + 2, :, :, 0, :, jl].reshape(256, D)
            dos = G[h, 0, 2 * t : 2 * t + 2, :, :, 1, :, jl].reshape(256, D)
            scores = dot(vkn[:, lanes], qs, NT) * KLOG
            top = jnp.max(scores, axis=0, keepdims=True)
            expo = jnp.exp2(scores - top)
            dprob = dot(vv[:, lanes], dos, NT)
            E[head, :, chunk] = expo
            DP[head, :, chunk] = dprob
            row = pl.ds(head, 1)
            ST[0, 0, row, chunk] = top
            ST[0, 1, row, chunk] = jnp.sum(expo, axis=0, keepdims=True)
            ST[0, 2, row, chunk] = jnp.sum(expo * dprob, axis=0, keepdims=True)

    def loop(body):
        def step(j, carry):
            body(j)
            return carry

        lax.fori_loop(0, 3, step, 0)

    loop(lambda j: first_pass(c, j))
    done(f0)
    done(f1)
    loop(lambda j: first_pass(o, j))

    def stats_start(level, to):
        return go(*[copy(ST.at[level], SR.at[level, k], one) for k, one in enumerate(to)])

    def stats_merge(level, copies):
        done(copies)
        tops = [ST[level, 0]] + [SR[level, k, 0] for k in range(3)]
        top = jnp.maximum(jnp.maximum(tops[0], tops[1]), jnp.maximum(tops[2], tops[3]))
        weights = [jnp.exp2(one - top) for one in tops]
        ST[level + 1, 0] = top
        for n in (1, 2):
            total = ST[level, n] * weights[0]
            for k in range(3):
                total = total + SR[level, k, n] * weights[k + 1]
            ST[level + 1, n] = total

    level0 = stats_start(0, (sib, opp, opp_sib))

    IA[...] = jnp.zeros_like(IA)

    def cross_slot(ch, j):
        return base_cross + 3 * ch + j

    base_cross = count[0]
    count[0] += 6

    def cross(ch, j):
        return copy(Xs.at[ch, j], Xr.at[ch, j], sib, slot=cross_slot(ch, j))

    def video_pass(h, j, own):
        head = 3 * h + j
        lanes, jl = lanes_of(head), lanes_of(j)
        keys = G[h, 1, :, :, :, 1, :, jl].reshape(TOK, D)
        values = G[h, 0, :, :, :, 0, :, jl].reshape(TOK, D)
        grad_k = grad_v = None
        for t in range(2):
            chunk = slice(256 * t, 256 * (t + 1))
            qs, dos = vqn[chunk, lanes], vdo[chunk, lanes]
            scores = dot(keys, qs, NT) * KLOG
            top = jnp.max(scores, axis=0, keepdims=True)
            expo = jnp.exp2(scores - top)
            probs = expo * (1.0 / jnp.sum(expo, axis=0, keepdims=True))
            low = probs.astype(BF16)
            dprob = dot(values, dos, NT)
            inner = jnp.sum(probs * dprob, axis=0, keepdims=True)
            ds = (probs * (dprob - inner)).astype(BF16)
            video_out[chunk, lanes] = dot(low, values, TN).astype(BF16)
            grad_q = dot(ds, keys, TN) * FACTOR
            GQ[chunk, lanes] = grad_q
            IA[0, chunk] += vq[chunk, lanes].astype(F32) * gvq_gain[:, lanes] * grad_q
            more_k, more_v = dot(ds, qs, NN), dot(low, dos, NN)
            grad_k = more_k if grad_k is None else grad_k + more_k
            grad_v = more_v if grad_v is None else grad_v + more_v
        put(0, h, j, own, slice(0, 4), 0, grad_k * FACTOR)
        put(0, h, j, own, slice(0, 4), 1, grad_v)

    def put(ch, h, j, own, chunks, a, value):
        rows = slice(128 * chunks.start, 128 * chunks.stop)
        if own:
            value = value + Xr[ch, j, a, rows].astype(F32)
            shape = (chunks.stop - chunks.start, 4, 2, 16, D)
            R[ch, chunks, :, :, a, :, lanes_of(j)] = value.reshape(shape).astype(BF16)
        else:
            Xs[ch, j, a, rows] = value.astype(BF16)

    def theirs(ch, work):
        def body(j):
            work(o, j, False)
            cross(ch, j).start()

        loop(body)

    def ours(ch, work):
        def body(j):
            cross(ch, j).wait()
            work(c, j, True)

        loop(body)

    theirs(0, video_pass)
    stats_merge(0, level0)
    level1 = stats_start(1, ring_p)
    ours(0, video_pass)
    stats_merge(1, level1)
    level2 = stats_start(2, ring_q)

    def rs_q1(ch):
        return go(
            copy(R.at[ch, q2, 0:2], RB1.at[ch, 0], right_q),
            copy(R.at[ch, q2, 2:4], RB1.at[ch, 1], left_q),
        )

    def rs_q2(ch, copies):
        done(copies)
        one = R[ch, qn, 0:2].astype(F32) + RB1[ch, 0].astype(F32)
        R[ch, qn, 0:2] = one.astype(BF16)
        two = R[ch, qb, 2:4].astype(F32) + RB1[ch, 1].astype(F32)
        R[ch, qb, 2:4] = two.astype(BF16)
        return go(
            copy(R.at[ch, qn], RB2.at[ch, 0], right_q),
            copy(R.at[ch, qb], RB2.at[ch, 1], left_q),
        )

    def rs_p(ch, copies):
        done(copies)
        total = R[ch, q].astype(F32) + RB2[ch, 0].astype(F32) + RB2[ch, 1].astype(F32)
        S[ch] = total.astype(BF16)
        return go(
            *[copy(S.at[ch, (p + k + 1) % 4], RB3.at[ch, k], ring_p[k]) for k in range(3)]
        )

    def rs_z(ch, copies):
        done(copies)
        total = S[ch, p].astype(F32)
        for k in range(3):
            total = total + RB3[ch, k].astype(F32)
        TZ[ch] = total.astype(BF16)
        return go(copy(TZ.at[ch, 1 - zh], RB4.at[ch], opp))

    def rs_core(ch, copies):
        done(copies)
        FS[ch] = TZ[ch, zh].astype(F32) + RB4[ch].astype(F32)
        theirs_rows = pl.ds(pl.multiple_of(o * 8, 8), 8)
        return go(copy(FS.at[ch, :, theirs_rows], FR.at[ch], sib))

    def rs_end(ch, copies, slots):
        done(copies)
        mine = pl.ds(pl.multiple_of(c * 8, 8), 8)
        for a, slot in enumerate(slots):
            sm[slot, :, my_half] = FS[ch, a, mine]
            sm[slot, :, its_half] = FR[ch, a]

    a1 = rs_q1(0)
    stats_merge(2, level2)

    total = ST[3, 1]
    safe = jnp.where(total == 0.0, 1.0, total)
    WT[0] = jnp.exp2(ST[0, 0] - ST[3, 0]) / safe
    WT[1] = ST[3, 2] / safe

    def second_pass(h, j, own):
        head = 3 * h + j
        lanes, jl = lanes_of(head), lanes_of(j)
        vks, vvs = vkn[:, lanes], vv[:, lanes]
        grad_k = grad_v = None
        for t in range(2):
            chunk = slice(256 * t, 256 * (t + 1))
            chunks = slice(2 * t, 2 * t + 2)
            row = pl.ds(head, 1)
            qs = G[h, 1, chunks, :, :, 0, :, jl].reshape(256, D)
            dos = G[h, 0, chunks, :, :, 1, :, jl].reshape(256, D)
            probs = E[head, :, chunk] * WT[0, row, chunk]
            low = probs.astype(BF16)
            ds = (probs * (DP[head, :, chunk] - WT[1, row, chunk])).astype(BF16)
            put(1, h, j, own, chunks, 0, dot(low, vvs, TN))
            put(1, h, j, own, chunks, 1, dot(ds, vks, TN) * FACTOR)
            more_k, more_v = dot(ds, qs, NN), dot(low, dos, NN)
            grad_k = more_k if grad_k is None else grad_k + more_k
            grad_v = more_v if grad_v is None else grad_v + more_v
        grad_k = grad_k * FACTOR
        out_gvv[:, lanes] = grad_v.astype(BF16)
        GK[:, lanes] = grad_k
        IA[1] += vk[:, lanes].astype(F32) * gvk_gain[:, lanes] * grad_k

    theirs(1, second_pass)
    a2 = rs_q2(0, a1)
    ours(1, second_pass)
    b1 = rs_q1(1)
    HI[hd] = jnp.zeros((8, 512), F32)
    HI[hd, 0:1, :] = row_of(IA[0])
    HI[hd, 1:2, :] = row_of(IA[1])
    inners = go(*[copy(HI.at[hd], HI.at[hd], to) for to in heads])
    a3 = rs_p(0, a2)
    b2 = rs_q2(1, b1)
    done(inners)
    inner = (HI[0] + HI[1] + HI[2] + HI[3]) / WIDTH

    def video_final(i, raw, gain, grad, out):
        inv_i = inv_col[i]
        scale = inv_i * inv_i * inv_i * col(inner[i : i + 1, :])
        for b in range(NH):
            at_b = slice(b * D, (b + 1) * D)
            value = inv_i * gain[:, at_b] * grad[:, at_b] - raw[:, at_b].astype(F32) * scale
            out[:, at_b] = value.astype(BF16)

    a4 = rs_z(0, a3)
    video_final(0, vq, gvq_gain, GQ, out_gvq)
    b3 = rs_p(1, b2)
    a5 = rs_core(0, a4)
    video_final(1, vk, gvk_gain, GK, out_gvk)
    b4 = rs_z(1, b3)
    rs_end(0, a5, (3, 4))
    b5 = rs_core(1, b4)
    rs_end(1, b5, (5, 2))
    parts = ((aq, gaq_gain, sm[2]), (ak, gak_gain, sm[3]))
    for i, (raw, gain, grad) in enumerate(parts):
        total = jnp.sum(raw[...].astype(F32) * gain[...] * grad, axis=1, keepdims=True)
        HA[hd, i] = jnp.broadcast_to(total, (8, D))
    small = go(*[copy(HA.at[hd], HA.at[hd], to) for to in heads])
    out_small[0] = sm[5]
    out_small[3] = sm[4]
    done(small)
    for i, (raw, gain, grad) in enumerate(parts):
        total = (HA[0, i] + HA[1, i] + HA[2, i] + HA[3, i]) / WIDTH
        wide = jnp.concatenate([inv_a[i]] * NH, axis=1)
        scale = jnp.concatenate([inv_a[i] * inv_a[i] * inv_a[i] * total] * NH, axis=1)
        out_small[1 + i] = wide * gain[...] * grad - raw[...].astype(F32) * scale


def shards(*args):
    arrays, gains = args[:8], [gain.reshape(1, LOCAL) for gain in args[8:]]
    big = jax.ShapeDtypeStruct((ROWS, LOCAL), BF16)
    vmem = pltpu.VMEM
    scratch = [
        vmem((2, 2, 4, 4, 2, 2, 16, HALF), BF16),
        vmem((2, 2, 8, HALF), F32),
        vmem((2, 2, 8, HALF), F32),
        vmem((4, 16, 512), F32),
        vmem((4, 8, 512), F32),
        vmem((4, 2, 8, D), F32),
        vmem((ROWS, LOCAL), BF16),
        vmem((ROWS, LOCAL), BF16),
        vmem((2, ROWS, D), F32),
        vmem((NH, ROWS, TOK), F32),
        vmem((NH, ROWS, TOK), F32),
        vmem((4, 3, 8, TOK), F32),
        vmem((3, 3, 3, 8, TOK), F32),
        vmem((2, 8, TOK), F32),
        vmem((ROWS, LOCAL), F32),
        vmem((ROWS, LOCAL), F32),
        vmem((2, ROWS, D), F32),
        vmem((2, 3, 2, TOK, D), BF16),
        vmem((2, 3, 2, TOK, D), BF16),
        vmem((2, 4, 4, 2, 2, 16, HALF), BF16),
        vmem((2, 2, 2, 2, 2, 16, HALF), BF16),
        vmem((2, 2, 4, 2, 2, 16, HALF), BF16),
        vmem((2, 4, 2, 2, 16, HALF), BF16),
        vmem((2, 3, 2, 2, 16, HALF), BF16),
        vmem((2, 2, 2, 16, HALF), BF16),
        vmem((2, 2, 16, HALF), BF16),
        vmem((2, 2, 16, HALF), F32),
        vmem((2, 2, 8, HALF), F32),
        vmem((6, 8, LOCAL), F32),
        pltpu.SemaphoreType.DMA((80,)),
        pltpu.SemaphoreType.DMA((80,)),
    ]
    spec = pl.BlockSpec(memory_space=pltpu.VMEM)
    made = pl.pallas_call(
        kernel,
        out_shape=(big, big, big, big, jax.ShapeDtypeStruct((4, 8, LOCAL), F32)),
        in_specs=[spec] * 12,
        out_specs=(spec,) * 5,
        scratch_shapes=scratch,
        compiler_params=pltpu.CompilerParams(
            collective_id=0, has_side_effects=True, vmem_limit_bytes=56 * 1024 * 1024
        ),
    )(*arrays, *gains)
    video_out, gvq, gvk, gvv, small = made
    small = small.astype(BF16)
    return video_out, small[0], gvq, gvk, gvv, small[1], small[2], small[3]


def solution(mesh):
    both = P("seq", "head")
    return jax.shard_map(
        shards,
        mesh=mesh,
        in_specs=(both,) * 8 + (P("head"),) * 4,
        out_specs=(both,) * 8,
        check_vma=False,
    )
```

time: 1740 us -> 104 us (0.06)
  blocking collectives: 1500 us -> 0 us
  waiting for transfers between devices: 133 us -> 0 us
  Pallas kernels: 0 us -> 92.2 us
  matrix products: 40.2 us -> 0 us
  local copies, waits for them, and re-layouts: 33.5 us -> 9.7 us
    all_gather x6 -> x0, blocking collectives: 698 us -> none  [the longest x1 121 us: shards(): lax.all_gather(normed[2], 'seq', axis=0, tiled=True)]
    unnamed x1 -> x0, blocking collectives: 390 us -> none
    pmax x1 -> x0, blocking collectives: 390 us -> none  [shards(): top_all = lax.pmax(jnp.max(scores_a, axis=2), 'seq')]
    reduce_scatter x3 -> x0, waiting for transfers between devices: 133 us -> none  [the longest x1 133 us: shards(): lax.psum_scatter((jnp.einsum('hqk,khd->qhd', ds_part, vk3, preferred_elem...]
    pallas_call x0 -> x1, Pallas kernels: none -> 92.2 us  [shards(): pl.pallas_call(kernel, out_shape=(big, big, big, big, jax.ShapeDtypeStruc...]
    dot_general x11 -> x0, matrix products: 35.4 us -> none  [the longest x1 5.22 us: shards(): jnp.einsum('hqk,khd->qhd', expo_a.astype(jnp.bfloat16), vv3, preferred_el...]
    psum x2 -> x0, blocking collectives: 19.2 us -> none  [the longest x1 11.9 us: shards(): lax.psum((square_sum(video_query), square_sum(video_key), square_sum(audi...]
    unnamed x83 -> x16, local copies, waits for them, and re-layouts: 25.1 us -> 6.07 us
  transfers between devices with their start and end apart: 3 -> 0, of which waited for: 1 -> 0; matrix products, arithmetic and copies ran while one was open for 3% -> 0% of each run, Pallas kernels for 0% -> 0%
where the time goes in v1:
time: 104 us; the launch traced here: 103 us
  Pallas kernels  92.2 us (89%)
  local copies, waits for them, and re-layouts  9.7 us (9%)
    pallas_call x1, Pallas kernels, shards(): pl.pallas_call(kernel, out_shape=(big, big, big, big, jax.ShapeDtypeStruc...  92.2 us
    unnamed x16, local copies, waits for them, and re-layouts  6.07 us
    reshape x4, local copies, waits for them, and re-layouts, shards(): arrays, gains = (args[:8], [gain.reshape(1, LOCAL) for gain in args[8:]])  3.01 us

profile of v1, /device:TPU:1, one launch (start us, length us, event | category | flops | bytes accessed | tf_op | source)
XLA Modules:
  0.0 103.4 jit_solution(14508123347508037392)
XLA Ops:
  0.6 0.0 copy-start.3
  0.6 1.3 %reshape.28.gvq_gain = f32[1,768]{1,0:T(1,128)} reshape(f32[768]{0:T(1024)} %param.20) | data formatting | bytes 6144 | tf_op jit(solution)/shard_map/reshape | solution.py:448
  1.9 0.0 copy-done.3
  1.9 0.0 copy-start.4
  1.9 0.6 reshape.29.gvk_gain
  2.5 0.1 copy-done.4
  2.6 0.0 copy-start.5
  2.6 0.6 reshape.30.gaq_gain
  3.2 0.1 copy-done.5
  3.3 0.6 reshape.31.gak_gain
  3.9 92.2 %shard_map.179 = (bf16[512,768]{1,0:T(8,128)(2,1)}, bf16[512,768]{1,0:T(8,128)(2,1)}, bf16[512,768]{1,0:T(8,128)(2,1)}, bf16[512,768]{1,0:T(8,128)(2,1)}, f32[4,8,768]{2,1,0:T(8,128)}) custom-call(bf16[512,768]{1,0:T(8,128)(2,1)} %vq.1, bf16[512,768]{1,0:T(8,128)(2,1)} %vk.1, bf16[512,768]{1,0:T(8,128)(2,1)} %vv.1, bf16[512,768]{1,0:T(8,128)(2,1)} %vdo.1, ...), custom_call_target="tpu_custom_call" | custom-call | tf_op jit(solution)/shard_map/pallas_call | solution.py:485
  96.1 0.9 convert_element_type.3
  97.0 0.6 slice_bitcast_fusion
  97.6 0.0 copy-start.2
  97.6 2.1 %copy.24 = bf16[512,768]{1,0:T(8,128)(2,1)} copy(bf16[512,768]{1,0:T(8,128)(2,1)} %get-tuple-element.30) | data formatting | bytes 1572864
  99.7 0.0 copy-done.2
  99.7 0.0 copy-start.1
  99.7 0.9 copy.25
  100.6 0.5 copy-done.1
  101.1 0.0 copy-start
  101.1 0.9 copy.26
  102.0 0.5 copy-done
  102.6 0.9 copy.27
Async XLA Ops:
  0.6 1.3 %copy-start.3 = (f32[768]{0:T(1024)S(1)}, f32[768]{0:T(1024)}, u32[]{:S(2)}) copy-start(f32[768]{0:T(1024)} %param.21) | copy-start | bytes 9220
  1.9 0.7 copy-start.4
  2.6 0.7 copy-start.5
  97.6 2.1 %copy-start.2 = (bf16[512,768]{1,0:T(8,128)(2,1)S(1)}, bf16[512,768]{1,0:T(8,128)(2,1)}, u32[]{:S(2)}) copy-start(bf16[512,768]{1,0:T(8,128)(2,1)} %get-tuple-element.32) | copy-start | bytes 2359300
  99.7 1.4 %copy-start.1 = (bf16[512,768]{1,0:T(8,128)(2,1)S(1)}, bf16[512,768]{1,0:T(8,128)(2,1)}, u32[]{:S(2)}) copy-start(bf16[512,768]{1,0:T(8,128)(2,1)} %get-tuple-element.33) | copy-start | bytes 2359300
  101.1 1.4 %copy-start = (bf16[512,768]{1,0:T(8,128)(2,1)S(1)}, bf16[512,768]{1,0:T(8,128)(2,1)}, u32[]{:S(2)}) copy-start(bf16[512,768]{1,0:T(8,128)(2,1)} %get-tuple-element.34) | copy-start | bytes 2359300

commit v2 on v1

v2 whole, which is shorter than its diff:
```python
import math

import jax
import jax.numpy as jnp
from jax import lax
from jax.experimental import pallas as pl
from jax.experimental.pallas import tpu as pltpu
from jax.sharding import PartitionSpec as P

HEADS = 24
D = 128
WIDTH = HEADS * D
EPS = 1e-06
FACTOR = 1.0 / math.sqrt(D)
KLOG = FACTOR * math.log2(math.e)
ROWS = 512
TOK = 512
LOCAL = 768
HALF = 384
NH = 6
F32 = jnp.float32
BF16 = jnp.bfloat16
MESH = pl.DeviceIdType.MESH
NT = (((1,), (1,)), ((), ()))
TN = (((0,), (0,)), ((), ()))
NN = (((1,), (0,)), ((), ()))


def dot(a, b, dims):
    return lax.dot_general(a, b, dims, preferred_element_type=F32)


def col(row):
    return jnp.transpose(jnp.broadcast_to(row, (D, ROWS)))


def row_of(square):
    return jnp.sum(jnp.transpose(square), axis=0, keepdims=True)


def kernel(
    vq_in, vk_in, vv_in, vdo_in, aq, ak, av, ado, gain0, gain1, gain2, gain3,
    video_out_hbm, gvq_hbm, gvk_hbm, gvv_hbm, out_small,
    vq, vk, vv, vdo, video_out, out_gvq, out_gvk, out_gvv, GN, RA,
    G, PK, PR, HSA, HS, HI, HAs, HAr, vqn, vkn, inv_col, E, DP, EV, DV, SV, ST, SR, WT,
    GQ, GK, IA, Xs, Xr, R, RB1, RB2, S, RB3, TZ, RB4, FS, FR, sm,
    send, recv, local,
):
    s = lax.axis_index("seq")
    hd = lax.axis_index("head")
    c = s % 2
    y = (s // 2) % 4
    x = (s // 8) % 4
    zh = s // 32
    p = x + c * (y - x)
    q = y + c * (x - y)
    o = 1 - c

    def at(zz, pp, qq):
        xx = pp + c * (qq - pp)
        yy = qq + c * (pp - qq)
        return {"seq": ((zz * 4 + xx) * 4 + yy) * 2 + c}

    sib = {"seq": s + 1 - 2 * c}
    opp = at(1 - zh, p, q)
    opp_sib = {"seq": s + 1 - 2 * c + 32 - 64 * zh}
    ring_p = [at(zh, (p + k) % 4, q) for k in (1, 2, 3)]
    ring_q = [at(zh, p, (q + k) % 4) for k in (1, 2, 3)]
    heads = [{"head": (hd + k) % 4} for k in (1, 2, 3)]
    heads_sib = [{"seq": s + 1 - 2 * c, "head": (hd + k) % 4} for k in (1, 2, 3)]
    pn, pb, p2 = (p + 1) % 4, (p + 3) % 4, (p + 2) % 4
    qn, qb, q2 = (q + 1) % 4, (q + 3) % 4, (q + 2) % 4
    right_q, left_q = ring_q[0], ring_q[2]

    barrier = pltpu.get_barrier_semaphore()
    partners = [sib, opp, opp_sib] + ring_p + ring_q + heads + heads_sib
    for partner in partners:
        pl.semaphore_signal(barrier, inc=1, device_id=partner, device_id_type=MESH)
    loads = [
        pltpu.make_async_copy(src, dst, local.at[i])
        for i, (src, dst) in enumerate(((vq_in, vq), (vk_in, vk), (vv_in, vv), (vdo_in, vdo)))
    ]
    for one in loads:
        one.start()
    for i, gain in enumerate((gain0, gain1, gain2, gain3)):
        GN[i : i + 1, :] = gain[...].reshape(1, LOCAL)
    gvq_gain, gvk_gain, gaq_gain, gak_gain = (GN.at[i : i + 1] for i in range(4))

    count = [0]

    def slots(n):
        first = count[0]
        count[0] += n
        return first

    def copy(src, dst, to, slot=None):
        slot = slots(1) if slot is None else slot
        return pltpu.make_async_remote_copy(
            src_ref=src,
            dst_ref=dst,
            send_sem=send.at[slot],
            recv_sem=recv.at[slot],
            device_id=to,
            device_id_type=MESH,
        )

    def go(*copies):
        for one in copies:
            one.start()
        return copies

    def done(copies):
        for one in copies:
            one.wait()

    half_of = [pl.ds(pl.multiple_of(i * HALF, D), HALF) for i in (c, o)]

    def pack(n, refs):
        for i, half in enumerate(half_of):
            rows = [ref[:, half].astype(F32) for ref in refs]
            PK[n, i] = jnp.concatenate(rows, axis=0).astype(BF16)

    def ag_first(n):
        return go(
            copy(PK.at[n, 1], PR.at[n, 0], sib),
            copy(PK.at[n, 0], PR.at[n, 1], opp),
            copy(PK.at[n, 1], PR.at[n, 2], opp_sib),
        )

    def chip_rows(mine, other, a):
        mine = mine.astype(F32)[8 * a : 8 * a + 8]
        other = other.astype(F32)[8 * a : 8 * a + 8]
        low = jnp.where(c == 0, mine, other)
        high = jnp.where(c == 0, other, mine)
        return jnp.concatenate([low, high], axis=0)

    def ag_p(ch, copies):
        done(copies)
        for a in range(2):
            G[c, ch, q, p, zh, a] = chip_rows(PK[ch, 0], PR[ch, 0], a).astype(BF16)
            G[c, ch, q, p, 1 - zh, a] = chip_rows(PR[ch, 1], PR[ch, 2], a).astype(BF16)
        block = G.at[c, ch, q, p]
        return go(*[copy(block, block, to) for to in ring_p])

    def forward(ch, i):
        block = G.at[c, ch, i]
        return go(copy(block, block, sib))

    def ag_q1(ch, copies):
        done(copies)
        block = G.at[c, ch, q]
        return go(copy(block, block, right_q), copy(block, block, left_q))

    def ag_q2(ch, copies):
        done(copies)
        one, two = G.at[c, ch, qb, 0:2], G.at[c, ch, qn, 2:4]
        return go(copy(one, one, right_q), copy(two, two, left_q))

    pack(0, (av, ado))
    for i, raw in enumerate((aq, ak)):
        block = raw[...].astype(F32)
        total = jnp.sum(block * block, axis=1, keepdims=True)
        HSA[hd, i] = jnp.broadcast_to(total, (8, D))
    pl.semaphore_wait(barrier, len(partners))
    sums_a = go(*[copy(HSA.at[hd], HSA.at[hd], to) for to in heads])
    first0 = ag_first(0)
    pack(2, (aq, ak))
    raws = go(copy(PK.at[2, 1], PR.at[2, 0], sib))

    HS[hd] = jnp.zeros((8, 512), F32)

    def video_sum(i, raw):
        loads[i].wait()
        total = jnp.zeros((ROWS, D), F32)
        for b in range(NH):
            block = raw[:, b * D : (b + 1) * D].astype(F32)
            total = total + block * block
        HS[hd, i : i + 1, :] = row_of(total)

    video_sum(0, vq)
    done(sums_a)
    inv_a = []
    for i, (raw, gain) in enumerate(((aq, gaq_gain), (ak, gak_gain))):
        total = HSA[0, i] + HSA[1, i] + HSA[2, i] + HSA[3, i]
        inv_a.append(lax.rsqrt(total / WIDTH + EPS))
        wide = jnp.concatenate([inv_a[i]] * NH, axis=1)
        sm[i] = (raw[...].astype(F32) * wide * gain[...]).astype(BF16).astype(F32)
    pack(1, (sm.at[0], sm.at[1]))
    first1 = ag_first(1)
    ring0 = ag_p(0, first0)
    video_sum(1, vk)
    sums = go(*[copy(HS.at[hd], HS.at[hd], to) for to in heads])
    ring1 = ag_p(1, first1)
    q10 = ag_q1(0, ring0)
    f0 = [forward(0, q)]
    done(sums)
    total = HS[0] + HS[1] + HS[2] + HS[3]
    inv = lax.rsqrt(total / WIDTH + EPS)

    def norm_video(i, raw, gain, out):
        inv_col[i] = col(inv[i : i + 1, :])
        for b in range(NH):
            at_b = slice(b * D, (b + 1) * D)
            out[:, at_b] = (raw[:, at_b].astype(F32) * inv_col[i] * gain[:, at_b]).astype(BF16)

    norm_video(1, vk, gvk_gain, vkn)
    q11 = ag_q1(1, ring1)
    f1 = [forward(1, q)]
    norm_video(0, vq, gvq_gain, vqn)

    def lanes_of(i):
        return pl.ds(pl.multiple_of(i * D, D), D)

    ST[...] = jnp.zeros_like(ST)

    def first_pass(h, j, i):
        head = 3 * h + j
        lanes, jl, chunk = lanes_of(head), lanes_of(j), lanes_of(i)
        keys = G[h, 1, i, :, :, 1, :, jl].reshape(D, D)
        values = G[h, 0, i, :, :, 0, :, jl].reshape(D, D)
        scores = dot(keys, vqn[:, lanes], NT) * KLOG
        top = jnp.max(scores, axis=0, keepdims=True)
        expo = jnp.exp2(scores - top)
        dprob = dot(values, vdo[:, lanes], NT)
        EV[head, chunk, :] = expo
        DV[head, chunk, :] = dprob
        row = pl.ds(i, 1)
        SV[0, head, row, :] = top
        SV[1, head, row, :] = jnp.sum(expo, axis=0, keepdims=True)
        SV[2, head, row, :] = jnp.sum(expo * dprob, axis=0, keepdims=True)
        qs = G[h, 1, i, :, :, 0, :, jl].reshape(D, D)
        dos = G[h, 0, i, :, :, 1, :, jl].reshape(D, D)
        scores = dot(vkn[:, lanes], qs, NT) * KLOG
        top = jnp.max(scores, axis=0, keepdims=True)
        expo = jnp.exp2(scores - top)
        dprob = dot(vv[:, lanes], dos, NT)
        E[head, :, chunk] = expo
        DP[head, :, chunk] = dprob
        row = pl.ds(head, 1)
        ST[0, 0, i, row, :] = top
        ST[0, 1, i, row, :] = jnp.sum(expo, axis=0, keepdims=True)
        ST[0, 2, i, row, :] = jnp.sum(expo * dprob, axis=0, keepdims=True)

    def loop(body):
        def step(j, carry):
            body(j)
            return carry

        lax.fori_loop(0, 3, step, 0)

    def first(h, *chunks):
        for i in chunks:
            loop(lambda j: first_pass(h, j, i))

    loads[2].wait()
    loads[3].wait()
    first(c, q)
    q20 = ag_q2(0, q10)
    f0 += [forward(0, qn), forward(0, qb)]
    q21 = ag_q2(1, q11)
    f1 += [forward(1, qn), forward(1, qb)]
    first(c, qn, qb)
    done(q20)
    f0.append(forward(0, q2))
    done(q21)
    f1.append(forward(1, q2))
    done(f0[0] + f1[0])
    first(o, p)
    first(c, q2)
    done(f0[1] + f1[1])
    first(o, pn)
    done(f0[2] + f1[2])
    first(o, pb)
    done(f0[3] + f1[3])
    first(o, p2)

    def stats_start(level, to):
        return go(*[copy(ST.at[level], SR.at[level, k], one) for k, one in enumerate(to)])

    def stats_merge(level, copies):
        done(copies)
        tops = [ST[level, 0]] + [SR[level, k, 0] for k in range(3)]
        top = jnp.maximum(jnp.maximum(tops[0], tops[1]), jnp.maximum(tops[2], tops[3]))
        weights = [jnp.exp2(one - top) for one in tops]
        ST[level + 1, 0] = top
        for n in (1, 2):
            total = ST[level, n] * weights[0]
            for k in range(3):
                total = total + SR[level, k, n] * weights[k + 1]
            ST[level + 1, n] = total

    level0 = stats_start(0, (sib, opp, opp_sib))
    done(raws)
    for i, gain in enumerate((gaq_gain, gak_gain)):
        RA[i] = chip_rows(PK[2, 0], PR[2, 0], i) * gain[:, half_of[0]]

    IA[...] = jnp.zeros_like(IA)
    base_cross = slots(6)

    def cross(ch, j):
        return copy(Xs.at[ch, j], Xr.at[ch, j], sib, slot=base_cross + 3 * ch + j)

    def put(ch, j, own, chunks, a, value):
        rows = slice(128 * chunks.start, 128 * chunks.stop)
        if own:
            value = value + Xr[ch, j, a, rows].astype(F32)
            shape = (chunks.stop - chunks.start, 4, 2, 16, D)
            R[ch, j, chunks, :, :, a] = value.reshape(shape).astype(BF16)
        else:
            Xs[ch, j, a, rows] = value.astype(BF16)

    def theirs(ch, work):
        def body(j):
            work(o, j, False)
            cross(ch, j).start()

        loop(body)

    def ours(ch, work):
        def body(j):
            cross(ch, j).wait()
            work(c, j, True)
            go(*rs_q1(ch, j))

        loop(body)

    base_q1 = slots(12)

    def rs_q1(ch, j):
        slot = base_q1 + 6 * ch + 2 * j
        return (
            copy(R.at[ch, j, q2, 0:2], RB1.at[ch, 0, j], right_q, slot=slot),
            copy(R.at[ch, j, q2, 2:4], RB1.at[ch, 1, j], left_q, slot=slot + 1),
        )

    def rs_q2(ch):
        copies = []
        for j in range(3):
            done(rs_q1(ch, j))
            one = R[ch, j, qn, 0:2].astype(F32) + RB1[ch, 0, j].astype(F32)
            R[ch, j, qn, 0:2] = one.astype(BF16)
            two = R[ch, j, qb, 2:4].astype(F32) + RB1[ch, 1, j].astype(F32)
            R[ch, j, qb, 2:4] = two.astype(BF16)
            copies += go(
                copy(R.at[ch, j, qn], RB2.at[ch, 0, j], right_q),
                copy(R.at[ch, j, qb], RB2.at[ch, 1, j], left_q),
            )
        return copies

    def rs_p(ch, copies):
        for j in range(3):
            done(copies[2 * j : 2 * j + 2])
            total = R[ch, j, q].astype(F32) + RB2[ch, 0, j].astype(F32) + RB2[ch, 1, j].astype(F32)
            S[ch, :, j] = total.astype(BF16)
        return go(
            *[copy(S.at[ch, (p + k + 1) % 4], RB3.at[ch, k], ring_p[k]) for k in range(3)]
        )

    def rs_z(ch, copies):
        done(copies)
        total = S[ch, p].astype(F32)
        for k in range(3):
            total = total + RB3[ch, k].astype(F32)
        low = total.astype(BF16)
        TZ[ch, 0] = low[:, 0]
        TZ[ch, 1] = low[:, 1]
        return go(copy(TZ.at[ch, 1 - zh], RB4.at[ch], opp))

    def rs_core(ch, copies):
        done(copies)
        total = TZ[ch, zh].astype(F32) + RB4[ch].astype(F32)
        for j in range(3):
            FS[ch, :, :, j * D : (j + 1) * D] = total[j]
        theirs_rows = pl.ds(pl.multiple_of(o * 8, 8), 8)
        rows = go(copy(FS.at[ch, :, theirs_rows], FR.at[ch], sib))
        total = jnp.sum(RA[1 - ch] * FS[ch, ch], axis=1, keepdims=True)
        HAs[ch] = jnp.broadcast_to(total, (16, D)).reshape(2, 8, D)
        HAr[ch, 2 * hd + c] = HAs[ch, c]
        mine, its = HAs.at[ch, c], HAs.at[ch, o]
        slot = HAr.at[ch, 2 * hd + c]
        rows += go(copy(its, slot, sib))
        rows += go(*[copy(mine, slot, to) for to in heads])
        rows += go(*[copy(its, slot, to) for to in heads_sib])
        return rows

    def rs_end(ch, copies, slots):
        done(copies)
        mine = pl.ds(pl.multiple_of(c * 8, 8), 8)
        for a, slot in enumerate(slots):
            sm[slot, :, half_of[0]] = FS[ch, a, mine]
            sm[slot, :, half_of[1]] = FR[ch, a]

    def video_pass(h, j, own):
        head = 3 * h + j
        lanes, jl = lanes_of(head), lanes_of(j)
        keys = G[h, 1, :, :, :, 1, :, jl].reshape(TOK, D)
        values = G[h, 0, :, :, :, 0, :, jl].reshape(TOK, D)
        tops = SV[0, head]
        weights = jnp.exp2(tops - jnp.max(tops, axis=0, keepdims=True))
        over = 1.0 / jnp.sum(weights * SV[1, head], axis=0, keepdims=True)
        weights = weights * over
        inner = jnp.sum(weights * SV[2, head], axis=0, keepdims=True)
        grad_k = grad_v = None
        for t in range(2):
            chunk = slice(256 * t, 256 * (t + 1))
            qs, dos = vqn[chunk, lanes], vdo[chunk, lanes]
            probs = jnp.concatenate(
                [EV[head, D * i : D * i + D, chunk] * weights[i : i + 1, chunk] for i in range(4)],
                axis=0,
            )
            low = probs.astype(BF16)
            ds = (probs * (DV[head, :, chunk] - inner[:, chunk])).astype(BF16)
            more_k, more_v = dot(ds, qs, NN), dot(low, dos, NN)
            grad_k = more_k if grad_k is None else grad_k + more_k
            grad_v = more_v if grad_v is None else grad_v + more_v
            video_out[chunk, lanes] = dot(low, values, TN).astype(BF16)
            grad_q = dot(ds, keys, TN) * FACTOR
            GQ[chunk, lanes] = grad_q
            IA[0, chunk] += vq[chunk, lanes].astype(F32) * gvq_gain[:, lanes] * grad_q
        put(0, j, own, slice(0, 4), 0, grad_k * FACTOR)
        put(0, j, own, slice(0, 4), 1, grad_v)

    def store(i, src, dst):
        one = pltpu.make_async_copy(src, dst, local.at[4 + i])
        one.start()
        return one

    def inner_start(i):
        HI[i, hd] = jnp.zeros((8, 512), F32)
        HI[i, hd, 0:1, :] = row_of(IA[i])
        return go(*[copy(HI.at[i, hd], HI.at[i, hd], to) for to in heads])

    def video_final(i, copies, raw, gain, grad, out):
        done(copies)
        inner = (HI[i, 0] + HI[i, 1] + HI[i, 2] + HI[i, 3]) / WIDTH
        inv_i = inv_col[i]
        scale = inv_i * inv_i * inv_i * col(inner[0:1, :])
        for b in range(NH):
            at_b = slice(b * D, (b + 1) * D)
            value = inv_i * gain[:, at_b] * grad[:, at_b] - raw[:, at_b].astype(F32) * scale
            out[:, at_b] = value.astype(BF16)

    theirs(0, video_pass)
    stats_merge(0, level0)
    level1 = stats_start(1, ring_p)
    ours(0, video_pass)
    stats_merge(1, level1)
    level2 = stats_start(2, ring_q)
    stores = [store(0, video_out, video_out_hbm)]
    inner0 = inner_start(0)
    a2 = rs_q2(0)
    stats_merge(2, level2)

    total = ST[3, 1]
    safe = jnp.where(total == 0.0, 1.0, total)
    WT[0] = jnp.exp2(ST[0, 0] - ST[3, 0]) / safe
    WT[1] = ST[3, 2] / safe

    def audio_probs(head, t):
        row = pl.ds(head, 1)
        weight, shift = (
            jnp.concatenate([WT[n, 2 * t, row, :], WT[n, 2 * t + 1, row, :]], axis=1)
            for n in (0, 1)
        )
        chunk = slice(256 * t, 256 * (t + 1))
        probs = E[head, :, chunk] * weight
        ds = (probs * (DP[head, :, chunk] - shift)).astype(BF16)
        return probs.astype(BF16), ds

    def audio_pass(h, j, own):
        head = 3 * h + j
        lanes = lanes_of(head)
        for t in range(2):
            low, ds = audio_probs(head, t)
            chunks = slice(2 * t, 2 * t + 2)
            put(1, j, own, chunks, 0, dot(low, vv[:, lanes], TN))
            put(1, j, own, chunks, 1, dot(ds, vkn[:, lanes], TN) * FACTOR)

    def row_pass(h, j):
        head = 3 * h + j
        lanes, jl = lanes_of(head), lanes_of(j)
        grad_k = grad_v = None
        for t in range(2):
            low, ds = audio_probs(head, t)
            chunks = slice(2 * t, 2 * t + 2)
            qs = G[h, 1, chunks, :, :, 0, :, jl].reshape(256, D)
            dos = G[h, 0, chunks, :, :, 1, :, jl].reshape(256, D)
            more_k, more_v = dot(ds, qs, NN), dot(low, dos, NN)
            grad_k = more_k if grad_k is None else grad_k + more_k
            grad_v = more_v if grad_v is None else grad_v + more_v
        grad_k = grad_k * FACTOR
        out_gvv[:, lanes] = grad_v.astype(BF16)
        GK[:, lanes] = grad_k
        IA[1] += vk[:, lanes].astype(F32) * gvk_gain[:, lanes] * grad_k

    theirs(1, audio_pass)
    ours(1, audio_pass)
    b2 = rs_q2(1)
    a3 = rs_p(0, a2)
    loop(lambda j: row_pass(0, j))
    b3 = rs_p(1, b2)
    a4 = rs_z(0, a3)
    loop(lambda j: row_pass(1, j))
    inner1 = inner_start(1)
    b4 = rs_z(1, b3)
    stores.append(store(1, out_gvv, gvv_hbm))
    a5 = rs_core(0, a4)
    video_final(0, inner0, vq, gvq_gain, GQ, out_gvq)
    stores.append(store(2, out_gvq, gvq_hbm))
    b5 = rs_core(1, b4)
    video_final(1, inner1, vk, gvk_gain, GK, out_gvk)
    stores.append(store(3, out_gvk, gvk_hbm))
    rs_end(0, a5, (3, 4))
    rs_end(1, b5, (5, 2))
    out_small[0] = sm[5]
    out_small[3] = sm[4]
    parts = ((aq, gaq_gain, sm[2]), (ak, gak_gain, sm[3]))
    for i, (raw, gain, grad) in enumerate(parts):
        total = HAr[1 - i, 0]
        for k in range(1, 8):
            total = total + HAr[1 - i, k]
        total = total / WIDTH
        wide = jnp.concatenate([inv_a[i]] * NH, axis=1)
        scale = jnp.concatenate([inv_a[i] * inv_a[i] * inv_a[i] * total] * NH, axis=1)
        out_small[1 + i] = wide * gain[...] * grad - raw[...].astype(F32) * scale
    for one in stores:
        one.wait()


def write_kernel(
    a, b, c, d, small, out_a, out_b, out_c, out_d, small_0, small_1, small_2, small_3, held, sems
):
    parts = ROWS // 2
    ins, outs = [], []
    for i, (src, dst) in enumerate(((a, out_a), (b, out_b), (c, out_c), (d, out_d))):
        for k in range(2):
            rows = slice(k * parts, (k + 1) * parts)
            n = 2 * i + k
            ins.append(pltpu.make_async_copy(src.at[rows], held.at[i, rows], sems.at[0, n]))
            outs.append(pltpu.make_async_copy(held.at[i, rows], dst.at[rows], sems.at[1, n]))
    for one in ins:
        one.start()
    for i, out in enumerate((small_0, small_1, small_2, small_3)):
        out[...] = small[i].astype(BF16)
    for one, two in zip(ins, outs):
        one.wait()
        two.start()
    for two in outs:
        two.wait()


def shards(*args):
    big = jax.ShapeDtypeStruct((ROWS, LOCAL), BF16)
    vmem = pltpu.VMEM
    wide = vmem((ROWS, LOCAL), BF16)
    scratch = [wide] * 8 + [
        vmem((8, LOCAL), F32),
        vmem((2, 16, HALF), F32),
        vmem((2, 2, 4, 4, 2, 2, 16, HALF), BF16),
        vmem((3, 2, 16, HALF), BF16),
        vmem((3, 3, 16, HALF), BF16),
        vmem((4, 2, 8, D), F32),
        vmem((4, 8, 512), F32),
        vmem((2, 4, 8, 512), F32),
        vmem((2, 2, 8, D), F32),
        vmem((2, 8, 8, D), F32),
        vmem((ROWS, LOCAL), BF16),
        vmem((ROWS, LOCAL), BF16),
        vmem((2, ROWS, D), F32),
        vmem((NH, ROWS, TOK), F32),
        vmem((NH, ROWS, TOK), F32),
        vmem((NH, TOK, ROWS), F32),
        vmem((NH, TOK, ROWS), F32),
        vmem((3, NH, 4, ROWS), F32),
        vmem((4, 3, 4, 8, D), F32),
        vmem((3, 3, 3, 4, 8, D), F32),
        vmem((2, 4, 8, D), F32),
        vmem((ROWS, LOCAL), F32),
        vmem((ROWS, LOCAL), F32),
        vmem((2, ROWS, D), F32),
        vmem((2, 3, 2, TOK, D), BF16),
        vmem((2, 3, 2, TOK, D), BF16),
        vmem((2, 3, 4, 4, 2, 2, 16, D), BF16),
        vmem((2, 2, 3, 2, 2, 2, 16, D), BF16),
        vmem((2, 2, 3, 4, 2, 2, 16, D), BF16),
        vmem((2, 4, 3, 2, 2, 16, D), BF16),
        vmem((2, 3, 3, 2, 2, 16, D), BF16),
        vmem((2, 2, 3, 2, 16, D), BF16),
        vmem((2, 3, 2, 16, D), BF16),
        vmem((2, 2, 16, HALF), F32),
        vmem((2, 2, 8, HALF), F32),
        vmem((6, 8, LOCAL), F32),
        pltpu.SemaphoreType.DMA((128,)),
        pltpu.SemaphoreType.DMA((128,)),
        pltpu.SemaphoreType.DMA((8,)),
    ]
    spec = pl.BlockSpec(memory_space=pltpu.VMEM)
    anywhere = pl.BlockSpec(memory_space=pl.ANY)
    made = pl.pallas_call(
        kernel,
        out_shape=(big, big, big, big, jax.ShapeDtypeStruct((4, 8, LOCAL), F32)),
        in_specs=[anywhere] * 4 + [spec] * 8,
        out_specs=(anywhere,) * 4 + (spec,),
        scratch_shapes=scratch,
        compiler_params=pltpu.CompilerParams(
            collective_id=0, has_side_effects=True, vmem_limit_bytes=60 * 1024 * 1024
        ),
    )(*args)
    small = jax.ShapeDtypeStruct((8, LOCAL), BF16)
    wrote = pl.pallas_call(
        write_kernel,
        out_shape=(big,) * 4 + (small,) * 4,
        in_specs=[anywhere] * 4 + [spec],
        out_specs=(anywhere,) * 4 + (spec,) * 4,
        scratch_shapes=[vmem((4, ROWS, LOCAL), BF16), pltpu.SemaphoreType.DMA((2, 8))],
    )(*made)
    video_out, gvq, gvk, gvv, audio_out, gaq, gak, gav = wrote
    return video_out, audio_out, gvq, gvk, gvv, gaq, gak, gav


def solution(mesh):
    both = P("seq", "head")
    return jax.shard_map(
        shards,
        mesh=mesh,
        in_specs=(both,) * 8 + (P("head"),) * 4,
        out_specs=(both,) * 8,
        check_vma=False,
    )
```

time: 104 us -> 87 us (0.84)
  local copies, waits for them, and re-layouts: 9.7 us -> 0 us
  Pallas kernels: 92.2 us -> 86.2 us
    pallas_call x1, Pallas kernels: 92.2 us -> 81.9 us  [shards(): pl.pallas_call(kernel, out_shape=(big, big, big, big, jax.ShapeDtypeStruc...]
    unnamed x16 -> x0, local copies, waits for them, and re-layouts: 6.07 us -> none
    pallas_call x0 -> x1, Pallas kernels: none -> 4.29 us  [shards(): pl.pallas_call(write_kernel, out_shape=(big,) * 4 + (small,) * 4, in_spec...]
    reshape x4 -> x0, local copies, waits for them, and re-layouts: 3.01 us -> none  [shards(): arrays, gains = (args[:8], [gain.reshape(1, LOCAL) for gain in args[8:]])]
where the time goes in v2:
time: 87 us; the launch traced here: 86.8 us
  Pallas kernels  86.2 us (99%)
    pallas_call x1, Pallas kernels, shards(): pl.pallas_call(kernel, out_shape=(big, big, big, big, jax.ShapeDtypeStruc...  81.9 us
    pallas_call x1, Pallas kernels, shards(): pl.pallas_call(write_kernel, out_shape=(big,) * 4 + (small,) * 4, in_spec...  4.29 us

profile of v2, /device:TPU:1, one launch (start us, length us, event | category | flops | bytes accessed | tf_op | source)
XLA Modules:
  0.0 86.8 jit_solution(16826758521484100231)
XLA Ops:
  0.6 81.9 %shard_map.179 = (bf16[512,768]{1,0:T(8,128)(2,1)}, bf16[512,768]{1,0:T(8,128)(2,1)}, bf16[512,768]{1,0:T(8,128)(2,1)}, bf16[512,768]{1,0:T(8,128)(2,1)}, f32[4,8,768]{2,1,0:T(8,128)}) custom-call(bf16[512,768]{1,0:T(8,128)(2,1)} %vq_in.1, bf16[512,768]{1,0:T(8,128)(2,1)} %vk_in.1, bf16[512,768]{1,0:T(8,128)(2,1)} %vv_in.1, bf16[512,768]{1,0:T(8,128)(2,1)} %vdo_in.1, ...), custom_call_target="tpu_custom_call" | custom-call | tf_op jit(solution)/shard_map/pallas_call | solution.py:599
  82.5 4.3 %shard_map.180 = (bf16[512,768]{1,0:T(8,128)(2,1)}, bf16[512,768]{1,0:T(8,128)(2,1)}, bf16[512,768]{1,0:T(8,128)(2,1)}, bf16[512,768]{1,0:T(8,128)(2,1)}, bf16[8...) custom-call(bf16[512,768]{1,0:T(8,128)(2,1)} %get-tuple-element.21.a, ...), custom_call_target="tpu_custom_call" | custom-call | tf_op jit(solution)/shard_map/pallas_call | solution.py:610

commit v3 on v2

--- a/solution.py
+++ b/solution.py
@@ -38,11 +38,20 @@
     return jnp.sum(jnp.transpose(square), axis=0, keepdims=True)
 
 
+def fold(op, array):
+    while array.shape[0] > 8:
+        half = array.shape[0] // 2
+        array = op(array[:half], array[half:])
+    if op is jnp.maximum:
+        return jnp.max(array, axis=0, keepdims=True)
+    return jnp.sum(array, axis=0, keepdims=True)
+
+
 def kernel(
     vq_in, vk_in, vv_in, vdo_in, aq, ak, av, ado, gain0, gain1, gain2, gain3,
     video_out_hbm, gvq_hbm, gvk_hbm, gvv_hbm, out_small,
     vq, vk, vv, vdo, video_out, out_gvq, out_gvk, out_gvv, GN, RA,
-    G, PK, PR, HSA, HS, HI, HAs, HAr, vqn, vkn, inv_col, E, DP, EV, DV, SV, ST, SR, WT,
+    G, PK, PR, HSA, HS, HI, HAs, HAr, vqn, vkn, vvT, vkT, inv_col, E, DP, EV, DV, SV, ST, SR, WT,
     GQ, GK, IA, Xs, Xr, R, RB1, RB2, S, RB3, TZ, RB4, FS, FR, sm,
     send, recv, local,
 ):
@@ -207,39 +216,46 @@
     q11 = ag_q1(1, ring1)
     f1 = [forward(1, q)]
     norm_video(0, vq, gvq_gain, vqn)
+    for b in range(NH):
+        at_b = slice(b * D, (b + 1) * D)
+        vkT[at_b, :] = jnp.transpose(vkn[:, at_b])
 
     def lanes_of(i):
         return pl.ds(pl.multiple_of(i * D, D), D)
 
     ST[...] = jnp.zeros_like(ST)
 
-    def first_pass(h, j, i):
+    def video_first(h, j, i):
         head = 3 * h + j
         lanes, jl, chunk = lanes_of(head), lanes_of(j), lanes_of(i)
         keys = G[h, 1, i, :, :, 1, :, jl].reshape(D, D)
         values = G[h, 0, i, :, :, 0, :, jl].reshape(D, D)
         scores = dot(keys, vqn[:, lanes], NT) * KLOG
-        top = jnp.max(scores, axis=0, keepdims=True)
+        dprob = dot(values, vdo[:, lanes], NT)
+        top = fold(jnp.maximum, scores)
         expo = jnp.exp2(scores - top)
-        dprob = dot(values, vdo[:, lanes], NT)
         EV[head, chunk, :] = expo
         DV[head, chunk, :] = dprob
         row = pl.ds(i, 1)
         SV[0, head, row, :] = top
-        SV[1, head, row, :] = jnp.sum(expo, axis=0, keepdims=True)
-        SV[2, head, row, :] = jnp.sum(expo * dprob, axis=0, keepdims=True)
+        SV[1, head, row, :] = fold(jnp.add, expo)
+        SV[2, head, row, :] = fold(jnp.add, expo * dprob)
+
+    def audio_first(h, j, i):
+        head = 3 * h + j
+        lanes, jl, chunk = lanes_of(head), lanes_of(j), lanes_of(i)
         qs = G[h, 1, i, :, :, 0, :, jl].reshape(D, D)
         dos = G[h, 0, i, :, :, 1, :, jl].reshape(D, D)
         scores = dot(vkn[:, lanes], qs, NT) * KLOG
-        top = jnp.max(scores, axis=0, keepdims=True)
+        dprob = dot(vv[:, lanes], dos, NT)
+        top = fold(jnp.maximum, scores)
         expo = jnp.exp2(scores - top)
-        dprob = dot(vv[:, lanes], dos, NT)
         E[head, :, chunk] = expo
         DP[head, :, chunk] = dprob
         row = pl.ds(head, 1)
         ST[0, 0, i, row, :] = top
-        ST[0, 1, i, row, :] = jnp.sum(expo, axis=0, keepdims=True)
-        ST[0, 2, i, row, :] = jnp.sum(expo * dprob, axis=0, keepdims=True)
+        ST[0, 1, i, row, :] = fold(jnp.add, expo)
+        ST[0, 2, i, row, :] = fold(jnp.add, expo * dprob)
 
     def loop(body):
         def step(j, carry):
@@ -248,31 +264,36 @@
 
         lax.fori_loop(0, 3, step, 0)
 
-    def first(h, *chunks):
+    def audio(h, *chunks):
         for i in chunks:
-            loop(lambda j: first_pass(h, j, i))
+            loop(lambda j: audio_first(h, j, i))
+
+    def video(h, *chunks):
+        for i in chunks:
+            loop(lambda j: video_first(h, j, i))
 
     loads[2].wait()
+    for b in range(NH):
+        at_b = slice(b * D, (b + 1) * D)
+        vvT[at_b, :] = jnp.transpose(vv[:, at_b])
+    audio(c, q)
     loads[3].wait()
-    first(c, q)
+    video(c, q)
     q20 = ag_q2(0, q10)
     f0 += [forward(0, qn), forward(0, qb)]
     q21 = ag_q2(1, q11)
     f1 += [forward(1, qn), forward(1, qb)]
-    first(c, qn, qb)
+    audio(c, qn, qb)
+    video(c, qn)
     done(q20)
     f0.append(forward(0, q2))
     done(q21)
     f1.append(forward(1, q2))
-    done(f0[0] + f1[0])
-    first(o, p)
-    first(c, q2)
-    done(f0[1] + f1[1])
-    first(o, pn)
-    done(f0[2] + f1[2])
-    first(o, pb)
-    done(f0[3] + f1[3])
-    first(o, p2)
+    video(c, qb)
+    audio(c, q2)
+    for n, i in enumerate((p, pn, pb, p2)):
+        done(f0[n] + f1[n])
+        audio(o, i)
 
     def stats_start(level, to):
         return go(*[copy(ST.at[level], SR.at[level, k], one) for k, one in enumerate(to)])
@@ -290,6 +311,8 @@
             ST[level + 1, n] = total
 
     level0 = stats_start(0, (sib, opp, opp_sib))
+    video(c, q2)
+    video(o, p, pn, pb, p2)
     done(raws)
     for i, gain in enumerate((gaq_gain, gak_gain)):
         RA[i] = chip_rows(PK[2, 0], PR[2, 0], i) * gain[:, half_of[0]]
@@ -390,35 +413,42 @@
             sm[slot, :, half_of[0]] = FS[ch, a, mine]
             sm[slot, :, half_of[1]] = FR[ch, a]
 
-    def video_pass(h, j, own):
-        head = 3 * h + j
-        lanes, jl = lanes_of(head), lanes_of(j)
-        keys = G[h, 1, :, :, :, 1, :, jl].reshape(TOK, D)
-        values = G[h, 0, :, :, :, 0, :, jl].reshape(TOK, D)
+    def video_probs(head):
         tops = SV[0, head]
         weights = jnp.exp2(tops - jnp.max(tops, axis=0, keepdims=True))
         over = 1.0 / jnp.sum(weights * SV[1, head], axis=0, keepdims=True)
         weights = weights * over
         inner = jnp.sum(weights * SV[2, head], axis=0, keepdims=True)
-        grad_k = grad_v = None
         for t in range(2):
             chunk = slice(256 * t, 256 * (t + 1))
-            qs, dos = vqn[chunk, lanes], vdo[chunk, lanes]
             probs = jnp.concatenate(
                 [EV[head, D * i : D * i + D, chunk] * weights[i : i + 1, chunk] for i in range(4)],
                 axis=0,
             )
-            low = probs.astype(BF16)
             ds = (probs * (DV[head, :, chunk] - inner[:, chunk])).astype(BF16)
-            more_k, more_v = dot(ds, qs, NN), dot(low, dos, NN)
+            yield chunk, probs.astype(BF16), ds
+
+    def video_pass(h, j, own):
+        head = 3 * h + j
+        lanes = lanes_of(head)
+        grad_k = grad_v = None
+        for chunk, low, ds in video_probs(head):
+            more_k, more_v = dot(ds, vqn[chunk, lanes], NN), dot(low, vdo[chunk, lanes], NN)
             grad_k = more_k if grad_k is None else grad_k + more_k
             grad_v = more_v if grad_v is None else grad_v + more_v
-            video_out[chunk, lanes] = dot(low, values, TN).astype(BF16)
-            grad_q = dot(ds, keys, TN) * FACTOR
+        put(0, j, own, slice(0, 4), 0, grad_k * FACTOR)
+        put(0, j, own, slice(0, 4), 1, grad_v)
+
+    def video_rows(h, j):
+        head = 3 * h + j
+        lanes, jl = lanes_of(head), lanes_of(j)
+        keys = jnp.transpose(G[h, 1, :, :, :, 1, :, jl].reshape(TOK, D))
+        values = jnp.transpose(G[h, 0, :, :, :, 0, :, jl].reshape(TOK, D))
+        for chunk, low, ds in video_probs(head):
+            video_out[chunk, lanes] = jnp.transpose(dot(values, low, NN)).astype(BF16)
+            grad_q = jnp.transpose(dot(keys, ds, NN)) * FACTOR
             GQ[chunk, lanes] = grad_q
             IA[0, chunk] += vq[chunk, lanes].astype(F32) * gvq_gain[:, lanes] * grad_q
-        put(0, j, own, slice(0, 4), 0, grad_k * FACTOR)
-        put(0, j, own, slice(0, 4), 1, grad_v)
 
     def store(i, src, dst):
         one = pltpu.make_async_copy(src, dst, local.at[4 + i])
@@ -446,8 +476,6 @@
     ours(0, video_pass)
     stats_merge(1, level1)
     level2 = stats_start(2, ring_q)
-    stores = [store(0, video_out, video_out_hbm)]
-    inner0 = inner_start(0)
     a2 = rs_q2(0)
     stats_merge(2, level2)
 
@@ -473,8 +501,8 @@
         for t in range(2):
             low, ds = audio_probs(head, t)
             chunks = slice(2 * t, 2 * t + 2)
-            put(1, j, own, chunks, 0, dot(low, vv[:, lanes], TN))
-            put(1, j, own, chunks, 1, dot(ds, vkn[:, lanes], TN) * FACTOR)
+            put(1, j, own, chunks, 0, jnp.transpose(dot(vvT[lanes, :], low, NN)))
+            put(1, j, own, chunks, 1, jnp.transpose(dot(vkT[lanes, :], ds, NN)) * FACTOR)
 
     def row_pass(h, j):
         head = 3 * h + j
@@ -497,17 +525,21 @@
     ours(1, audio_pass)
     b2 = rs_q2(1)
     a3 = rs_p(0, a2)
-    loop(lambda j: row_pass(0, j))
+    loop(lambda j: video_rows(0, j))
     b3 = rs_p(1, b2)
     a4 = rs_z(0, a3)
+    loop(lambda j: video_rows(1, j))
+    inner0 = inner_start(0)
+    stores = [store(0, video_out, video_out_hbm)]
+    b4 = rs_z(1, b3)
+    a5 = rs_core(0, a4)
+    loop(lambda j: row_pass(0, j))
     loop(lambda j: row_pass(1, j))
     inner1 = inner_start(1)
-    b4 = rs_z(1, b3)
     stores.append(store(1, out_gvv, gvv_hbm))
-    a5 = rs_core(0, a4)
+    b5 = rs_core(1, b4)
     video_final(0, inner0, vq, gvq_gain, GQ, out_gvq)
     stores.append(store(2, out_gvq, gvq_hbm))
-    b5 = rs_core(1, b4)
     video_final(1, inner1, vk, gvk_gain, GK, out_gvk)
     stores.append(store(3, out_gvk, gvk_hbm))
     rs_end(0, a5, (3, 4))
@@ -530,12 +562,12 @@
 def write_kernel(
     a, b, c, d, small, out_a, out_b, out_c, out_d, small_0, small_1, small_2, small_3, held, sems
 ):
-    parts = ROWS // 2
+    parts = ROWS // 4
     ins, outs = [], []
     for i, (src, dst) in enumerate(((a, out_a), (b, out_b), (c, out_c), (d, out_d))):
-        for k in range(2):
+        for k in range(4):
             rows = slice(k * parts, (k + 1) * parts)
-            n = 2 * i + k
+            n = 4 * i + k
             ins.append(pltpu.make_async_copy(src.at[rows], held.at[i, rows], sems.at[0, n]))
             outs.append(pltpu.make_async_copy(held.at[i, rows], dst.at[rows], sems.at[1, n]))
     for one in ins:
@@ -566,6 +598,8 @@
         vmem((2, 8, 8, D), F32),
         vmem((ROWS, LOCAL), BF16),
         vmem((ROWS, LOCAL), BF16),
+        vmem((LOCAL, ROWS), BF16),
+        vmem((LOCAL, ROWS), BF16),
         vmem((2, ROWS, D), F32),
         vmem((NH, ROWS, TOK), F32),
         vmem((NH, ROWS, TOK), F32),
@@ -612,7 +646,7 @@
         out_shape=(big,) * 4 + (small,) * 4,
         in_specs=[anywhere] * 4 + [spec],
         out_specs=(anywhere,) * 4 + (spec,) * 4,
-        scratch_shapes=[vmem((4, ROWS, LOCAL), BF16), pltpu.SemaphoreType.DMA((2, 8))],
+        scratch_shapes=[vmem((4, ROWS, LOCAL), BF16), pltpu.SemaphoreType.DMA((2, 16))],
     )(*made)
     video_out, gvq, gvk, gvv, audio_out, gaq, gak, gav = wrote
     return video_out, audio_out, gvq, gvk, gvv, gaq, gak, gav

time: 87 us -> 88.5 us (1.017)
  Pallas kernels: 86.2 us -> 87.7 us
    pallas_call x1, Pallas kernels: 81.9 us -> 83 us  [shards(): pl.pallas_call(kernel, out_shape=(big, big, big, big, jax.ShapeDtypeStruc...]
where the time goes in v3:
time: 88.5 us; the launch traced here: 88.4 us
  Pallas kernels  87.7 us (99%)
    pallas_call x1, Pallas kernels, shards(): pl.pallas_call(kernel, out_shape=(big, big, big, big, jax.ShapeDtypeStruc...  83 us
    pallas_call x1, Pallas kernels, shards(): pl.pallas_call(write_kernel, out_shape=(big,) * 4 + (small,) * 4, in_spec...  4.68 us

profile of v3, /device:TPU:1, one launch (start us, length us, event | category | flops | bytes accessed | tf_op | source)
XLA Modules:
  0.0 88.4 jit_solution(12130661369180977785)
XLA Ops:
  0.6 83.0 %shard_map.179 = (bf16[512,768]{1,0:T(8,128)(2,1)}, bf16[512,768]{1,0:T(8,128)(2,1)}, bf16[512,768]{1,0:T(8,128)(2,1)}, bf16[512,768]{1,0:T(8,128)(2,1)}, f32[4,8,768]{2,1,0:T(8,128)}) custom-call(bf16[512,768]{1,0:T(8,128)(2,1)} %vq_in.1, bf16[512,768]{1,0:T(8,128)(2,1)} %vk_in.1, bf16[512,768]{1,0:T(8,128)(2,1)} %vv_in.1, bf16[512,768]{1,0:T(8,128)(2,1)} %vdo_in.1, ...), custom_call_target="tpu_custom_call" | custom-call | tf_op jit(solution)/shard_map/pallas_call | solution.py:633
  83.7 4.7 %shard_map.180 = (bf16[512,768]{1,0:T(8,128)(2,1)}, bf16[512,768]{1,0:T(8,128)(2,1)}, bf16[512,768]{1,0:T(8,128)(2,1)}, bf16[512,768]{1,0:T(8,128)(2,1)}, bf16[8...) custom-call(bf16[512,768]{1,0:T(8,128)(2,1)} %get-tuple-element.21.a, ...), custom_call_target="tpu_custom_call" | custom-call | tf_op jit(solution)/shard_map/pallas_call | solution.py:644

commit v4 on v3

--- a/solution.py
+++ b/solution.py
@@ -151,9 +151,12 @@
         block = G.at[c, ch, q, p]
         return go(*[copy(block, block, to) for to in ring_p])
 
-    def forward(ch, i):
+    base_f = slots(8)
+
+    def forward(ch, n):
+        i = (q + n + (n // 2) * (5 - 2 * n)) % 4
         block = G.at[c, ch, i]
-        return go(copy(block, block, sib))
+        return copy(block, block, sib, slot=base_f + 4 * ch + n)
 
     def ag_q1(ch, copies):
         done(copies)
@@ -201,7 +204,7 @@
     sums = go(*[copy(HS.at[hd], HS.at[hd], to) for to in heads])
     ring1 = ag_p(1, first1)
     q10 = ag_q1(0, ring0)
-    f0 = [forward(0, q)]
+    go(forward(0, 0))
     done(sums)
     total = HS[0] + HS[1] + HS[2] + HS[3]
     inv = lax.rsqrt(total / WIDTH + EPS)
@@ -214,7 +217,7 @@
 
     norm_video(1, vk, gvk_gain, vkn)
     q11 = ag_q1(1, ring1)
-    f1 = [forward(1, q)]
+    go(forward(1, 0))
     norm_video(0, vq, gvq_gain, vqn)
     for b in range(NH):
         at_b = slice(b * D, (b + 1) * D)
@@ -225,52 +228,73 @@
 
     ST[...] = jnp.zeros_like(ST)
 
-    def video_first(h, j, i):
-        head = 3 * h + j
-        lanes, jl, chunk = lanes_of(head), lanes_of(j), lanes_of(i)
-        keys = G[h, 1, i, :, :, 1, :, jl].reshape(D, D)
-        values = G[h, 0, i, :, :, 0, :, jl].reshape(D, D)
-        scores = dot(keys, vqn[:, lanes], NT) * KLOG
-        dprob = dot(values, vdo[:, lanes], NT)
-        top = fold(jnp.maximum, scores)
-        expo = jnp.exp2(scores - top)
-        EV[head, chunk, :] = expo
-        DV[head, chunk, :] = dprob
-        row = pl.ds(i, 1)
-        SV[0, head, row, :] = top
-        SV[1, head, row, :] = fold(jnp.add, expo)
-        SV[2, head, row, :] = fold(jnp.add, expo * dprob)
-
-    def audio_first(h, j, i):
-        head = 3 * h + j
-        lanes, jl, chunk = lanes_of(head), lanes_of(j), lanes_of(i)
-        qs = G[h, 1, i, :, :, 0, :, jl].reshape(D, D)
-        dos = G[h, 0, i, :, :, 1, :, jl].reshape(D, D)
-        scores = dot(vkn[:, lanes], qs, NT) * KLOG
-        dprob = dot(vv[:, lanes], dos, NT)
-        top = fold(jnp.maximum, scores)
-        expo = jnp.exp2(scores - top)
-        E[head, :, chunk] = expo
-        DP[head, :, chunk] = dprob
-        row = pl.ds(head, 1)
-        ST[0, 0, i, row, :] = top
-        ST[0, 1, i, row, :] = fold(jnp.add, expo)
-        ST[0, 2, i, row, :] = fold(jnp.add, expo * dprob)
-
-    def loop(body):
-        def step(j, carry):
-            body(j)
+    def staged(units, make, use):
+        held = None
+        for unit in units:
+            made = make(unit)
+            if held is not None:
+                use(*held)
+            held = (unit, made)
+        use(*held)
+
+    def rows_of(ch, h, i, a, j):
+        return G[h, ch, i, :, :, a, :, j * D : j * D + D].reshape(D, D)
+
+    def some_rows(ch, h, ids, a, j):
+        return jnp.concatenate([rows_of(ch, h, i, a, j) for i in ids], axis=0)
+
+    def video(h, *ids):
+        def make(j):
+            lanes = lanes_of(3 * h + j)
+            scores = dot(some_rows(1, h, ids, 1, j), vqn[:, lanes], NT) * KLOG
+            return scores, dot(some_rows(0, h, ids, 0, j), vdo[:, lanes], NT)
+
+        def use(j, made):
+            scores, dprob = made
+            head = 3 * h + j
+            top = fold(jnp.maximum, scores)
+            expo = jnp.exp2(scores - top)
+            nothing = jnp.zeros_like(top)
+            values = [top, fold(jnp.add, expo), fold(jnp.add, expo * dprob)]
+            for n, i in enumerate(ids):
+                part = slice(D * n, D * n + D)
+                EV[head, lanes_of(i), :] = expo[part]
+                DV[head, lanes_of(i), :] = dprob[part]
+                for k in range(3):
+                    SV[k, head, pl.ds(i, 1), :] = nothing if n and k else values[k]
+
+        staged(range(3), make, use)
+
+    def audio(h, *ids):
+        def make(j):
+            lanes = lanes_of(3 * h + j)
+            scores = dot(vkn[:, lanes], some_rows(1, h, ids, 0, j), NT) * KLOG
+            return scores, dot(vv[:, lanes], some_rows(0, h, ids, 1, j), NT)
+
+        def use(j, made):
+            scores, dprob = made
+            head = 3 * h + j
+            top = fold(jnp.maximum, scores)
+            expo = jnp.exp2(scores - top)
+            values = [top, fold(jnp.add, expo), fold(jnp.add, expo * dprob)]
+            for n, i in enumerate(ids):
+                part = slice(D * n, D * n + D)
+                E[head, :, lanes_of(i)] = expo[:, part]
+                DP[head, :, lanes_of(i)] = dprob[:, part]
+                for k in range(3):
+                    ST[0, k, i, pl.ds(head, 1), :] = values[k][:, part]
+
+        staged(range(3), make, use)
+
+    def pair(n):
+        return (p + 3 * n) % 4, (p + 1 + n) % 4
+
+    def twice(body):
+        def step(n, carry):
+            body(n)
             return carry
 
-        lax.fori_loop(0, 3, step, 0)
-
-    def audio(h, *chunks):
-        for i in chunks:
-            loop(lambda j: audio_first(h, j, i))
-
-    def video(h, *chunks):
-        for i in chunks:
-            loop(lambda j: video_first(h, j, i))
+        lax.fori_loop(0, 2, step, 0)
 
     loads[2].wait()
     for b in range(NH):
@@ -280,20 +304,22 @@
     loads[3].wait()
     video(c, q)
     q20 = ag_q2(0, q10)
-    f0 += [forward(0, qn), forward(0, qb)]
+    go(*[forward(0, n) for n in (1, 2)])
     q21 = ag_q2(1, q11)
-    f1 += [forward(1, qn), forward(1, qb)]
+    go(*[forward(1, n) for n in (1, 2)])
     audio(c, qn, qb)
-    video(c, qn)
     done(q20)
-    f0.append(forward(0, q2))
+    go(forward(0, 3))
     done(q21)
-    f1.append(forward(1, q2))
-    video(c, qb)
+    go(forward(1, 3))
+    video(c, qn, qb)
     audio(c, q2)
-    for n, i in enumerate((p, pn, pb, p2)):
-        done(f0[n] + f1[n])
-        audio(o, i)
+
+    def their_audio(n):
+        done([forward(ch, 2 * n + k) for ch in range(2) for k in range(2)])
+        audio(o, *pair(n))
+
+    twice(their_audio)
 
     def stats_start(level, to):
         return go(*[copy(ST.at[level], SR.at[level, k], one) for k, one in enumerate(to)])
@@ -312,7 +338,7 @@
 
     level0 = stats_start(0, (sib, opp, opp_sib))
     video(c, q2)
-    video(o, p, pn, pb, p2)
+    twice(lambda n: video(o, *pair(n)))
     done(raws)
     for i, gain in enumerate((gaq_gain, gak_gain)):
         RA[i] = chip_rows(PK[2, 0], PR[2, 0], i) * gain[:, half_of[0]]
@@ -331,21 +357,6 @@
             R[ch, j, chunks, :, :, a] = value.reshape(shape).astype(BF16)
         else:
             Xs[ch, j, a, rows] = value.astype(BF16)
-
-    def theirs(ch, work):
-        def body(j):
-            work(o, j, False)
-            cross(ch, j).start()
-
-        loop(body)
-
-    def ours(ch, work):
-        def body(j):
-            cross(ch, j).wait()
-            work(c, j, True)
-            go(*rs_q1(ch, j))
-
-        loop(body)
 
     base_q1 = slots(12)
 
@@ -413,42 +424,59 @@
             sm[slot, :, half_of[0]] = FS[ch, a, mine]
             sm[slot, :, half_of[1]] = FR[ch, a]
 
-    def video_probs(head):
+    units = [(j, t) for j in range(3) for t in range(2)]
+
+    def video_probs(h, part):
+        j, t = part
+        head = 3 * h + j
         tops = SV[0, head]
         weights = jnp.exp2(tops - jnp.max(tops, axis=0, keepdims=True))
         over = 1.0 / jnp.sum(weights * SV[1, head], axis=0, keepdims=True)
         weights = weights * over
         inner = jnp.sum(weights * SV[2, head], axis=0, keepdims=True)
-        for t in range(2):
-            chunk = slice(256 * t, 256 * (t + 1))
-            probs = jnp.concatenate(
-                [EV[head, D * i : D * i + D, chunk] * weights[i : i + 1, chunk] for i in range(4)],
-                axis=0,
-            )
-            ds = (probs * (DV[head, :, chunk] - inner[:, chunk])).astype(BF16)
-            yield chunk, probs.astype(BF16), ds
-
-    def video_pass(h, j, own):
-        head = 3 * h + j
-        lanes = lanes_of(head)
-        grad_k = grad_v = None
-        for chunk, low, ds in video_probs(head):
-            more_k, more_v = dot(ds, vqn[chunk, lanes], NN), dot(low, vdo[chunk, lanes], NN)
-            grad_k = more_k if grad_k is None else grad_k + more_k
-            grad_v = more_v if grad_v is None else grad_v + more_v
-        put(0, j, own, slice(0, 4), 0, grad_k * FACTOR)
-        put(0, j, own, slice(0, 4), 1, grad_v)
-
-    def video_rows(h, j):
-        head = 3 * h + j
-        lanes, jl = lanes_of(head), lanes_of(j)
-        keys = jnp.transpose(G[h, 1, :, :, :, 1, :, jl].reshape(TOK, D))
-        values = jnp.transpose(G[h, 0, :, :, :, 0, :, jl].reshape(TOK, D))
-        for chunk, low, ds in video_probs(head):
+        chunk = slice(256 * t, 256 * (t + 1))
+        probs = jnp.concatenate(
+            [EV[head, D * i : D * i + D, chunk] * weights[i : i + 1, chunk] for i in range(4)],
+            axis=0,
+        )
+        ds = (probs * (DV[head, :, chunk] - inner[:, chunk])).astype(BF16)
+        return probs.astype(BF16), ds
+
+    def finish(ch, j, own):
+        go(*(rs_q1(ch, j) if own else (cross(ch, j),)))
+
+    def video_pass(h, own):
+        sums = {}
+
+        def use(part, made):
+            j, t = part
+            low, ds = made
+            chunk, lanes = slice(256 * t, 256 * (t + 1)), lanes_of(3 * h + j)
+            grads = dot(ds, vqn[chunk, lanes], NN), dot(low, vdo[chunk, lanes], NN)
+            if t == 0:
+                sums[j] = grads
+                return
+            if own:
+                cross(0, j).wait()
+            put(0, j, own, slice(0, 4), 0, (sums[j][0] + grads[0]) * FACTOR)
+            put(0, j, own, slice(0, 4), 1, sums[j][1] + grads[1])
+            finish(0, j, own)
+
+        staged(units, lambda part: video_probs(h, part), use)
+
+    def video_rows(h):
+        def use(part, made):
+            j, t = part
+            low, ds = made
+            chunk, lanes = slice(256 * t, 256 * (t + 1)), lanes_of(3 * h + j)
+            keys = jnp.transpose(some_rows(1, h, range(4), 1, j))
+            values = jnp.transpose(some_rows(0, h, range(4), 0, j))
             video_out[chunk, lanes] = jnp.transpose(dot(values, low, NN)).astype(BF16)
             grad_q = jnp.transpose(dot(keys, ds, NN)) * FACTOR
             GQ[chunk, lanes] = grad_q
             IA[0, chunk] += vq[chunk, lanes].astype(F32) * gvq_gain[:, lanes] * grad_q
+
+        staged(units, lambda part: video_probs(h, part), use)
 
     def store(i, src, dst):
         one = pltpu.make_async_copy(src, dst, local.at[4 + i])
@@ -470,10 +498,10 @@
             value = inv_i * gain[:, at_b] * grad[:, at_b] - raw[:, at_b].astype(F32) * scale
             out[:, at_b] = value.astype(BF16)
 
-    theirs(0, video_pass)
+    video_pass(o, False)
     stats_merge(0, level0)
     level1 = stats_start(1, ring_p)
-    ours(0, video_pass)
+    video_pass(c, True)
     stats_merge(1, level1)
     level2 = stats_start(2, ring_q)
     a2 = rs_q2(0)
@@ -484,7 +512,9 @@
     WT[0] = jnp.exp2(ST[0, 0] - ST[3, 0]) / safe
     WT[1] = ST[3, 2] / safe
 
-    def audio_probs(head, t):
+    def audio_probs(h, part):
+        j, t = part
+        head = 3 * h + j
         row = pl.ds(head, 1)
         weight, shift = (
             jnp.concatenate([WT[n, 2 * t, row, :], WT[n, 2 * t + 1, row, :]], axis=1)
@@ -495,46 +525,55 @@
         ds = (probs * (DP[head, :, chunk] - shift)).astype(BF16)
         return probs.astype(BF16), ds
 
-    def audio_pass(h, j, own):
-        head = 3 * h + j
-        lanes = lanes_of(head)
-        for t in range(2):
-            low, ds = audio_probs(head, t)
+    def audio_pass(h, own):
+        def use(part, made):
+            j, t = part
+            low, ds = made
+            lanes = lanes_of(3 * h + j)
             chunks = slice(2 * t, 2 * t + 2)
-            put(1, j, own, chunks, 0, jnp.transpose(dot(vvT[lanes, :], low, NN)))
-            put(1, j, own, chunks, 1, jnp.transpose(dot(vkT[lanes, :], ds, NN)) * FACTOR)
-
-    def row_pass(h, j):
-        head = 3 * h + j
-        lanes, jl = lanes_of(head), lanes_of(j)
-        grad_k = grad_v = None
-        for t in range(2):
-            low, ds = audio_probs(head, t)
-            chunks = slice(2 * t, 2 * t + 2)
-            qs = G[h, 1, chunks, :, :, 0, :, jl].reshape(256, D)
-            dos = G[h, 0, chunks, :, :, 1, :, jl].reshape(256, D)
-            more_k, more_v = dot(ds, qs, NN), dot(low, dos, NN)
-            grad_k = more_k if grad_k is None else grad_k + more_k
-            grad_v = more_v if grad_v is None else grad_v + more_v
-        grad_k = grad_k * FACTOR
-        out_gvv[:, lanes] = grad_v.astype(BF16)
-        GK[:, lanes] = grad_k
-        IA[1] += vk[:, lanes].astype(F32) * gvk_gain[:, lanes] * grad_k
-
-    theirs(1, audio_pass)
-    ours(1, audio_pass)
+            numer = jnp.transpose(dot(vvT[lanes, :], low, NN))
+            grad_q = jnp.transpose(dot(vkT[lanes, :], ds, NN)) * FACTOR
+            if own and t == 0:
+                cross(1, j).wait()
+            put(1, j, own, chunks, 0, numer)
+            put(1, j, own, chunks, 1, grad_q)
+            if t == 1:
+                finish(1, j, own)
+
+        staged(units, lambda part: audio_probs(h, part), use)
+
+    def row_pass(h):
+        sums = {}
+
+        def use(part, made):
+            j, t = part
+            low, ds = made
+            lanes = lanes_of(3 * h + j)
+            ids = (2 * t, 2 * t + 1)
+            grads = dot(ds, some_rows(1, h, ids, 0, j), NN), dot(low, some_rows(0, h, ids, 1, j), NN)
+            if t == 0:
+                sums[j] = grads
+                return
+            grad_k = (sums[j][0] + grads[0]) * FACTOR
+            out_gvv[:, lanes] = (sums[j][1] + grads[1]).astype(BF16)
+            GK[:, lanes] = grad_k
+            IA[1] += vk[:, lanes].astype(F32) * gvk_gain[:, lanes] * grad_k
+
+        staged(units, lambda part: audio_probs(h, part), use)
+
+    audio_pass(o, False)
+    audio_pass(c, True)
     b2 = rs_q2(1)
     a3 = rs_p(0, a2)
-    loop(lambda j: video_rows(0, j))
+    video_rows(0)
     b3 = rs_p(1, b2)
     a4 = rs_z(0, a3)
-    loop(lambda j: video_rows(1, j))
+    video_rows(1)
     inner0 = inner_start(0)
     stores = [store(0, video_out, video_out_hbm)]
     b4 = rs_z(1, b3)
     a5 = rs_core(0, a4)
-    loop(lambda j: row_pass(0, j))
-    loop(lambda j: row_pass(1, j))
+    twice(row_pass)
     inner1 = inner_start(1)
     stores.append(store(1, out_gvv, gvv_hbm))
     b5 = rs_core(1, b4)

time: 88.5 us -> 86 us (0.972)
  Pallas kernels: 87.7 us -> 85 us
    pallas_call x1, Pallas kernels: 83 us -> 80.3 us  [shards(): pl.pallas_call(kernel, out_shape=(big, big, big, big, jax.ShapeDtypeStruc...]
where the time goes in v4:
time: 86 us; the launch traced here: 85.8 us
  Pallas kernels  85 us (99%)
    pallas_call x1, Pallas kernels, shards(): pl.pallas_call(kernel, out_shape=(big, big, big, big, jax.ShapeDtypeStruc...  80.3 us
    pallas_call x1, Pallas kernels, shards(): pl.pallas_call(write_kernel, out_shape=(big,) * 4 + (small,) * 4, in_spec...  4.68 us

profile of v4, /device:TPU:1, one launch (start us, length us, event | category | flops | bytes accessed | tf_op | source)
XLA Modules:
  0.0 85.8 jit_solution(11891396369989553057)
XLA Ops:
  0.6 80.3 %shard_map.179 = (bf16[512,768]{1,0:T(8,128)(2,1)}, bf16[512,768]{1,0:T(8,128)(2,1)}, bf16[512,768]{1,0:T(8,128)(2,1)}, bf16[512,768]{1,0:T(8,128)(2,1)}, f32[4,8,768]{2,1,0:T(8,128)}) custom-call(bf16[512,768]{1,0:T(8,128)(2,1)} %vq_in.1, bf16[512,768]{1,0:T(8,128)(2,1)} %vk_in.1, bf16[512,768]{1,0:T(8,128)(2,1)} %vv_in.1, bf16[512,768]{1,0:T(8,128)(2,1)} %vdo_in.1, ...), custom_call_target="tpu_custom_call" | custom-call | tf_op jit(solution)/shard_map/pallas_call | solution.py:672
  81.0 4.7 %shard_map.180 = (bf16[512,768]{1,0:T(8,128)(2,1)}, bf16[512,768]{1,0:T(8,128)(2,1)}, bf16[512,768]{1,0:T(8,128)(2,1)}, bf16[512,768]{1,0:T(8,128)(2,1)}, bf16[8...) custom-call(bf16[512,768]{1,0:T(8,128)(2,1)} %get-tuple-element.21.a, ...), custom_call_target="tpu_custom_call" | custom-call | tf_op jit(solution)/shard_map/pallas_call | solution.py:683

commit v5 on v4

--- a/solution.py
+++ b/solution.py
@@ -49,10 +49,10 @@
 
 def kernel(
     vq_in, vk_in, vv_in, vdo_in, aq, ak, av, ado, gain0, gain1, gain2, gain3,
-    video_out_hbm, gvq_hbm, gvk_hbm, gvv_hbm, out_small,
-    vq, vk, vv, vdo, video_out, out_gvq, out_gvk, out_gvv, GN, RA,
+    video_out, out_gvq, out_gvk, out_gvv, out_small,
+    vq, vk, vv, vdo, GN, RA,
     G, PK, PR, HSA, HS, HI, HAs, HAr, vqn, vkn, vvT, vkT, inv_col, E, DP, EV, DV, SV, ST, SR, WT,
-    GQ, GK, IA, Xs, Xr, R, RB1, RB2, S, RB3, TZ, RB4, FS, FR, sm,
+    GQ, GK, IA, Xs, Xr, R, RB1, RB2, S, RB3, TF, TZ, RB4, sm,
     send, recv, local,
 ):
     s = lax.axis_index("seq")
@@ -76,13 +76,14 @@
     ring_p = [at(zh, (p + k) % 4, q) for k in (1, 2, 3)]
     ring_q = [at(zh, p, (q + k) % 4) for k in (1, 2, 3)]
     heads = [{"head": (hd + k) % 4} for k in (1, 2, 3)]
-    heads_sib = [{"seq": s + 1 - 2 * c, "head": (hd + k) % 4} for k in (1, 2, 3)]
+    near = [sib, opp, opp_sib]
+    far = [[dict(to, head=(hd + k) % 4) for k in (1, 2, 3)] for to in near]
     pn, pb, p2 = (p + 1) % 4, (p + 3) % 4, (p + 2) % 4
     qn, qb, q2 = (q + 1) % 4, (q + 3) % 4, (q + 2) % 4
     right_q, left_q = ring_q[0], ring_q[2]
 
     barrier = pltpu.get_barrier_semaphore()
-    partners = [sib, opp, opp_sib] + ring_p + ring_q + heads + heads_sib
+    partners = near + ring_p + ring_q + heads + far[0] + far[1] + far[2]
     for partner in partners:
         pl.semaphore_signal(barrier, inc=1, device_id=partner, device_id_type=MESH)
     loads = [
@@ -177,7 +178,7 @@
     sums_a = go(*[copy(HSA.at[hd], HSA.at[hd], to) for to in heads])
     first0 = ag_first(0)
     pack(2, (aq, ak))
-    raws = go(copy(PK.at[2, 1], PR.at[2, 0], sib))
+    raws = ag_first(2)
 
     HS[hd] = jnp.zeros((8, 512), F32)
 
@@ -341,7 +342,8 @@
     twice(lambda n: video(o, *pair(n)))
     done(raws)
     for i, gain in enumerate((gaq_gain, gak_gain)):
-        RA[i] = chip_rows(PK[2, 0], PR[2, 0], i) * gain[:, half_of[0]]
+        RA[zh, i] = chip_rows(PK[2, 0], PR[2, 0], i) * gain[:, half_of[0]]
+        RA[1 - zh, i] = chip_rows(PR[2, 1], PR[2, 2], i) * gain[:, half_of[0]]
 
     IA[...] = jnp.zeros_like(IA)
     base_cross = slots(6)
@@ -390,39 +392,39 @@
             *[copy(S.at[ch, (p + k + 1) % 4], RB3.at[ch, k], ring_p[k]) for k in range(3)]
         )
 
-    def rs_z(ch, copies):
+    def rs_last(ch, copies):
         done(copies)
         total = S[ch, p].astype(F32)
         for k in range(3):
             total = total + RB3[ch, k].astype(F32)
-        low = total.astype(BF16)
-        TZ[ch, 0] = low[:, 0]
-        TZ[ch, 1] = low[:, 1]
-        return go(copy(TZ.at[ch, 1 - zh], RB4.at[ch], opp))
-
-    def rs_core(ch, copies):
-        done(copies)
-        total = TZ[ch, zh].astype(F32) + RB4[ch].astype(F32)
-        for j in range(3):
-            FS[ch, :, :, j * D : (j + 1) * D] = total[j]
-        theirs_rows = pl.ds(pl.multiple_of(o * 8, 8), 8)
-        rows = go(copy(FS.at[ch, :, theirs_rows], FR.at[ch], sib))
-        total = jnp.sum(RA[1 - ch] * FS[ch, ch], axis=1, keepdims=True)
-        HAs[ch] = jnp.broadcast_to(total, (16, D)).reshape(2, 8, D)
-        HAr[ch, 2 * hd + c] = HAs[ch, c]
-        mine, its = HAs.at[ch, c], HAs.at[ch, o]
-        slot = HAr.at[ch, 2 * hd + c]
-        rows += go(copy(its, slot, sib))
-        rows += go(*[copy(mine, slot, to) for to in heads])
-        rows += go(*[copy(its, slot, to) for to in heads_sib])
-        return rows
+        for zz in range(2):
+            both = [jnp.concatenate([total[j, zz, a] for j in range(3)], axis=1) for a in range(2)]
+            for cc in range(2):
+                rows = slice(8 * cc, 8 * cc + 8)
+                tile = jnp.concatenate([both[0][rows], both[1][rows]], axis=0)
+                TF[ch, zz, cc] = tile
+                TZ[ch, zz, cc] = tile.astype(BF16)
+            inner = jnp.sum(RA[zz, 1 - ch] * both[ch], axis=1, keepdims=True)
+            HAs[ch, zz] = jnp.broadcast_to(inner, (16, D)).reshape(2, 8, D)
+        place = ((zh, c), (zh, o), (1 - zh, c), (1 - zh, o))
+        rows = go(
+            *[copy(TZ.at[ch, zz, cc], RB4.at[ch, k], near[k]) for k, (zz, cc) in enumerate(place[1:])]
+        )
+        sender = 4 * hd + 2 * zh + c
+        slot = HAr.at[ch, sender]
+        HAr[ch, sender] = HAs[ch, zh, c]
+        targets = [(place[0], to) for to in heads]
+        for k in range(3):
+            targets += [(place[k + 1], to) for to in [near[k]] + far[k]]
+        return rows + go(*[copy(HAs.at[ch, zz, cc], slot, to) for (zz, cc), to in targets])
 
     def rs_end(ch, copies, slots):
         done(copies)
-        mine = pl.ds(pl.multiple_of(c * 8, 8), 8)
+        mine = TF[ch, zh, c] + RB4[ch, 1].astype(F32)
+        other = RB4[ch, 0].astype(F32) + RB4[ch, 2].astype(F32)
         for a, slot in enumerate(slots):
-            sm[slot, :, half_of[0]] = FS[ch, a, mine]
-            sm[slot, :, half_of[1]] = FR[ch, a]
+            sm[slot, :, half_of[0]] = mine[8 * a : 8 * a + 8]
+            sm[slot, :, half_of[1]] = other[8 * a : 8 * a + 8]
 
     units = [(j, t) for j in range(3) for t in range(2)]
 
@@ -478,11 +480,6 @@
 
         staged(units, lambda part: video_probs(h, part), use)
 
-    def store(i, src, dst):
-        one = pltpu.make_async_copy(src, dst, local.at[4 + i])
-        one.start()
-        return one
-
     def inner_start(i):
         HI[i, hd] = jnp.zeros((8, 512), F32)
         HI[i, hd, 0:1, :] = row_of(IA[i])
@@ -504,7 +501,10 @@
     video_pass(c, True)
     stats_merge(1, level1)
     level2 = stats_start(2, ring_q)
+    video_rows(0)
     a2 = rs_q2(0)
+    video_rows(1)
+    inner0 = inner_start(0)
     stats_merge(2, level2)
 
     total = ST[3, 1]
@@ -562,79 +562,64 @@
         staged(units, lambda part: audio_probs(h, part), use)
 
     audio_pass(o, False)
+    a3 = rs_p(0, a2)
     audio_pass(c, True)
     b2 = rs_q2(1)
-    a3 = rs_p(0, a2)
-    video_rows(0)
+    a4 = rs_last(0, a3)
+    row_pass(0)
     b3 = rs_p(1, b2)
-    a4 = rs_z(0, a3)
-    video_rows(1)
-    inner0 = inner_start(0)
-    stores = [store(0, video_out, video_out_hbm)]
-    b4 = rs_z(1, b3)
-    a5 = rs_core(0, a4)
-    twice(row_pass)
+    row_pass(1)
     inner1 = inner_start(1)
-    stores.append(store(1, out_gvv, gvv_hbm))
-    b5 = rs_core(1, b4)
+    b4 = rs_last(1, b3)
     video_final(0, inner0, vq, gvq_gain, GQ, out_gvq)
-    stores.append(store(2, out_gvq, gvq_hbm))
     video_final(1, inner1, vk, gvk_gain, GK, out_gvk)
-    stores.append(store(3, out_gvk, gvk_hbm))
-    rs_end(0, a5, (3, 4))
-    rs_end(1, b5, (5, 2))
+    rs_end(0, a4, (3, 4))
+    rs_end(1, b4, (5, 2))
     out_small[0] = sm[5]
     out_small[3] = sm[4]
     parts = ((aq, gaq_gain, sm[2]), (ak, gak_gain, sm[3]))
     for i, (raw, gain, grad) in enumerate(parts):
         total = HAr[1 - i, 0]
-        for k in range(1, 8):
+        for k in range(1, 16):
             total = total + HAr[1 - i, k]
         total = total / WIDTH
         wide = jnp.concatenate([inv_a[i]] * NH, axis=1)
         scale = jnp.concatenate([inv_a[i] * inv_a[i] * inv_a[i] * total] * NH, axis=1)
         out_small[1 + i] = wide * gain[...] * grad - raw[...].astype(F32) * scale
-    for one in stores:
-        one.wait()
 
 
 def write_kernel(
-    a, b, c, d, small, out_a, out_b, out_c, out_d, small_0, small_1, small_2, small_3, held, sems
+    a, b, c, d, small, out_a, out_b, out_c, out_d, small_0, small_1, small_2, small_3, sems
 ):
     parts = ROWS // 4
-    ins, outs = [], []
+    copies = []
     for i, (src, dst) in enumerate(((a, out_a), (b, out_b), (c, out_c), (d, out_d))):
         for k in range(4):
             rows = slice(k * parts, (k + 1) * parts)
-            n = 4 * i + k
-            ins.append(pltpu.make_async_copy(src.at[rows], held.at[i, rows], sems.at[0, n]))
-            outs.append(pltpu.make_async_copy(held.at[i, rows], dst.at[rows], sems.at[1, n]))
-    for one in ins:
+            copies.append(pltpu.make_async_copy(src.at[rows], dst.at[rows], sems.at[4 * i + k]))
+    for one in copies:
         one.start()
     for i, out in enumerate((small_0, small_1, small_2, small_3)):
         out[...] = small[i].astype(BF16)
-    for one, two in zip(ins, outs):
+    for one in copies:
         one.wait()
-        two.start()
-    for two in outs:
-        two.wait()
 
 
 def shards(*args):
     big = jax.ShapeDtypeStruct((ROWS, LOCAL), BF16)
     vmem = pltpu.VMEM
     wide = vmem((ROWS, LOCAL), BF16)
-    scratch = [wide] * 8 + [
+    scratch = [wide] * 4 + [
         vmem((8, LOCAL), F32),
-        vmem((2, 16, HALF), F32),
+        vmem((2, 2, 16, HALF), F32),
         vmem((2, 2, 4, 4, 2, 2, 16, HALF), BF16),
         vmem((3, 2, 16, HALF), BF16),
         vmem((3, 3, 16, HALF), BF16),
         vmem((4, 2, 8, D), F32),
         vmem((4, 8, 512), F32),
         vmem((2, 4, 8, 512), F32),
-        vmem((2, 2, 8, D), F32),
-        vmem((2, 8, 8, D), F32),
+        vmem((2, 2, 2, 8, D), F32),
+        vmem((2, 16, 8, D), F32),
         vmem((ROWS, LOCAL), BF16),
         vmem((ROWS, LOCAL), BF16),
         vmem((LOCAL, ROWS), BF16),
@@ -658,34 +643,33 @@
         vmem((2, 2, 3, 4, 2, 2, 16, D), BF16),
         vmem((2, 4, 3, 2, 2, 16, D), BF16),
         vmem((2, 3, 3, 2, 2, 16, D), BF16),
-        vmem((2, 2, 3, 2, 16, D), BF16),
-        vmem((2, 3, 2, 16, D), BF16),
-        vmem((2, 2, 16, HALF), F32),
-        vmem((2, 2, 8, HALF), F32),
+        vmem((2, 2, 2, 16, HALF), F32),
+        vmem((2, 2, 2, 16, HALF), BF16),
+        vmem((2, 3, 16, HALF), BF16),
         vmem((6, 8, LOCAL), F32),
-        pltpu.SemaphoreType.DMA((128,)),
-        pltpu.SemaphoreType.DMA((128,)),
+        pltpu.SemaphoreType.DMA((160,)),
+        pltpu.SemaphoreType.DMA((160,)),
         pltpu.SemaphoreType.DMA((8,)),
     ]
     spec = pl.BlockSpec(memory_space=pltpu.VMEM)
     anywhere = pl.BlockSpec(memory_space=pl.ANY)
     made = pl.pallas_call(
         kernel,
-        out_shape=(big, big, big, big, jax.ShapeDtypeStruct((4, 8, LOCAL), F32)),
+        out_shape=(vmem((ROWS, LOCAL), BF16),) * 4 + (vmem((4, 8, LOCAL), F32),),
         in_specs=[anywhere] * 4 + [spec] * 8,
-        out_specs=(anywhere,) * 4 + (spec,),
+        out_specs=(spec,) * 5,
         scratch_shapes=scratch,
         compiler_params=pltpu.CompilerParams(
-            collective_id=0, has_side_effects=True, vmem_limit_bytes=60 * 1024 * 1024
+            collective_id=0, has_side_effects=True, vmem_limit_bytes=57 * 1024 * 1024
         ),
     )(*args)
     small = jax.ShapeDtypeStruct((8, LOCAL), BF16)
     wrote = pl.pallas_call(
         write_kernel,
         out_shape=(big,) * 4 + (small,) * 4,
-        in_specs=[anywhere] * 4 + [spec],
+        in_specs=[spec] * 5,
         out_specs=(anywhere,) * 4 + (spec,) * 4,
-        scratch_shapes=[vmem((4, ROWS, LOCAL), BF16), pltpu.SemaphoreType.DMA((2, 16))],
+        scratch_shapes=[pltpu.SemaphoreType.DMA((16,))],
     )(*made)
     video_out, gvq, gvk, gvv, audio_out, gaq, gak, gav = wrote
     return video_out, audio_out, gvq, gvk, gvv, gaq, gak, gav

time: 86 us -> 88.8 us (1.033)
  local copies, waits for them, and re-layouts: 0 us -> 4.2 us
  Pallas kernels: 85 us -> 83.7 us
    unnamed x0 -> x10, local copies, waits for them, and re-layouts: none -> 4.2 us
    pallas_call x1, Pallas kernels: 80.3 us -> 79.4 us  [shards(): pl.pallas_call(kernel, out_shape=(vmem((ROWS, LOCAL), BF16),) * 4 + (vmem...]
where the time goes in v5:
time: 88.8 us; the launch traced here: 88.7 us
  Pallas kernels  83.7 us (94%)
  local copies, waits for them, and re-layouts  4.2 us (5%)
    pallas_call x1, Pallas kernels, shards(): pl.pallas_call(kernel, out_shape=(vmem((ROWS, LOCAL), BF16),) * 4 + (vmem...  79.4 us
    pallas_call x1, Pallas kernels, shards(): pl.pallas_call(write_kernel, out_shape=(big,) * 4 + (small,) * 4, in_spec...  4.24 us
    unnamed x10, local copies, waits for them, and re-layouts  4.2 us

profile of v5, /device:TPU:1, one launch (start us, length us, event | category | flops | bytes accessed | tf_op | source)
XLA Modules:
  0.0 88.7 jit_solution(11789679087562626235)
XLA Ops:
  0.6 79.4 %shard_map.179 = (bf16[512,768]{1,0:T(8,128)(2,1)S(1)}, bf16[512,768]{1,0:T(8,128)(2,1)S(1)}, bf16[512,768]{1,0:T(8,128)(2,1)S(1)}, bf16[512,768]{1,0:T(8,128)(2,1)S(1)}, f32[4,8,768]{2,1,0:T(8,128)S(1)}) custom-call(bf16[512,768]{1,0:T(8,128)(2,1)} %vq_in.1, bf16[512,768]{1,0:T(8,128)(2,1)} %vk_in.1, bf16[512,768]{1,0:T(8,128)(2,1)} %vv_in.1, ...), custom_call_target="tpu_custom_call" | custom-call | tf_op jit(solution)/shard_map/pallas_call | solution.py:656
  80.1 0.0 copy-start
  80.1 0.9 copy-done
  81.0 0.0 copy-start.1
  81.0 0.9 copy-done.1
  81.9 0.0 copy-start.2
  81.9 0.9 %copy-done.2 = bf16[512,768]{1,0:T(8,128)(2,1)} copy-done((bf16[512,768]{1,0:T(8,128)(2,1)}, bf16[512,768]{1,0:T(8,128)(2,1)S(1)}, u32[]{:S(2)}) %copy-start.2) | copy-done | bytes 786456
  82.8 0.0 copy-start.3
  82.8 0.9 %copy-done.3 = bf16[512,768]{1,0:T(8,128)(2,1)} copy-done((bf16[512,768]{1,0:T(8,128)(2,1)}, bf16[512,768]{1,0:T(8,128)(2,1)S(1)}, u32[]{:S(2)}) %copy-start.3) | copy-done | bytes 786456
  83.6 0.0 copy-start.4
  83.6 0.6 copy-done.4
  84.3 4.2 %shard_map.180 = (bf16[512,768]{1,0:T(8,128)(2,1)}, bf16[512,768]{1,0:T(8,128)(2,1)}, bf16[512,768]{1,0:T(8,128)(2,1)}, bf16[512,768]{1,0:T(8,128)(2,1)}, bf16[8...) custom-call(bf16[512,768]{1,0:T(8,128)(2,1)} %copy-done, ...), custom_call_target="tpu_custom_call" | custom-call | tf_op jit(solution)/shard_map/pallas_call | solution.py:667
Async XLA Ops:
  80.1 0.9 %copy-start = (bf16[512,768]{1,0:T(8,128)(2,1)}, bf16[512,768]{1,0:T(8,128)(2,1)S(1)}, u32[]{:S(2)}) copy-start(bf16[512,768]{1,0:T(8,128)(2,1)S(1)} %get-tuple-element.21.a) | copy-start | bytes 2359300
  81.0 0.9 %copy-start.1 = (bf16[512,768]{1,0:T(8,128)(2,1)}, bf16[512,768]{1,0:T(8,128)(2,1)S(1)}, u32[]{:S(2)}) copy-start(bf16[512,768]{1,0:T(8,128)(2,1)S(1)} %get-tuple-element.22.b) | copy-start | bytes 2359300
  81.9 0.9 %copy-start.2 = (bf16[512,768]{1,0:T(8,128)(2,1)}, bf16[512,768]{1,0:T(8,128)(2,1)S(1)}, u32[]{:S(2)}) copy-start(bf16[512,768]{1,0:T(8,128)(2,1)S(1)} %get-tuple-element.23.c) | copy-start | bytes 2359300
  82.8 0.9 %copy-start.3 = (bf16[512,768]{1,0:T(8,128)(2,1)}, bf16[512,768]{1,0:T(8,128)(2,1)S(1)}, u32[]{:S(2)}) copy-start(bf16[512,768]{1,0:T(8,128)(2,1)S(1)} %get-tuple-element.24.d) | copy-start | bytes 2359300
  83.6 0.6 copy-start.4

commit v6 on v5

--- a/solution.py
+++ b/solution.py
@@ -369,9 +369,9 @@
             copy(R.at[ch, j, q2, 2:4], RB1.at[ch, 1, j], left_q, slot=slot + 1),
         )
 
-    def rs_q2(ch):
+    def rs_q2(ch, heads_done):
         copies = []
-        for j in range(3):
+        for j in heads_done:
             done(rs_q1(ch, j))
             one = R[ch, j, qn, 0:2].astype(F32) + RB1[ch, 0, j].astype(F32)
             R[ch, j, qn, 0:2] = one.astype(BF16)
@@ -456,27 +456,21 @@
             chunk, lanes = slice(256 * t, 256 * (t + 1)), lanes_of(3 * h + j)
             grads = dot(ds, vqn[chunk, lanes], NN), dot(low, vdo[chunk, lanes], NN)
             if t == 0:
-                sums[j] = grads
+                keys = jnp.transpose(some_rows(1, h, range(4), 1, j))
+                values = jnp.transpose(some_rows(0, h, range(4), 0, j))
+                sums[j] = grads + (keys, values)
+            keys, values = sums[j][2:]
+            video_out[chunk, lanes] = jnp.transpose(dot(values, low, NN)).astype(BF16)
+            grad_q = jnp.transpose(dot(keys, ds, NN)) * FACTOR
+            GQ[chunk, lanes] = grad_q
+            IA[0, chunk] += vq[chunk, lanes].astype(F32) * gvq_gain[:, lanes] * grad_q
+            if t == 0:
                 return
             if own:
                 cross(0, j).wait()
             put(0, j, own, slice(0, 4), 0, (sums[j][0] + grads[0]) * FACTOR)
             put(0, j, own, slice(0, 4), 1, sums[j][1] + grads[1])
             finish(0, j, own)
-
-        staged(units, lambda part: video_probs(h, part), use)
-
-    def video_rows(h):
-        def use(part, made):
-            j, t = part
-            low, ds = made
-            chunk, lanes = slice(256 * t, 256 * (t + 1)), lanes_of(3 * h + j)
-            keys = jnp.transpose(some_rows(1, h, range(4), 1, j))
-            values = jnp.transpose(some_rows(0, h, range(4), 0, j))
-            video_out[chunk, lanes] = jnp.transpose(dot(values, low, NN)).astype(BF16)
-            grad_q = jnp.transpose(dot(keys, ds, NN)) * FACTOR
-            GQ[chunk, lanes] = grad_q
-            IA[0, chunk] += vq[chunk, lanes].astype(F32) * gvq_gain[:, lanes] * grad_q
 
         staged(units, lambda part: video_probs(h, part), use)
 
@@ -495,15 +489,12 @@
             value = inv_i * gain[:, at_b] * grad[:, at_b] - raw[:, at_b].astype(F32) * scale
             out[:, at_b] = value.astype(BF16)
 
-    video_pass(o, False)
     stats_merge(0, level0)
     level1 = stats_start(1, ring_p)
-    video_pass(c, True)
+    video_pass(o, False)
     stats_merge(1, level1)
     level2 = stats_start(2, ring_q)
-    video_rows(0)
-    a2 = rs_q2(0)
-    video_rows(1)
+    video_pass(c, True)
     inner0 = inner_start(0)
     stats_merge(2, level2)
 
@@ -562,13 +553,15 @@
         staged(units, lambda part: audio_probs(h, part), use)
 
     audio_pass(o, False)
+    a2 = rs_q2(0, (0, 1, 2))
+    audio_pass(c, True)
+    b2 = rs_q2(1, (0,))
     a3 = rs_p(0, a2)
-    audio_pass(c, True)
-    b2 = rs_q2(1)
+    row_pass(0)
+    b2 += rs_q2(1, (1, 2))
     a4 = rs_last(0, a3)
-    row_pass(0)
+    row_pass(1)
     b3 = rs_p(1, b2)
-    row_pass(1)
     inner1 = inner_start(1)
     b4 = rs_last(1, b3)
     video_final(0, inner0, vq, gvq_gain, GQ, out_gvq)
@@ -670,7 +663,8 @@
         in_specs=[spec] * 5,
         out_specs=(anywhere,) * 4 + (spec,) * 4,
         scratch_shapes=[pltpu.SemaphoreType.DMA((16,))],
-    )(*made)
+        compiler_params=pltpu.CompilerParams(vmem_limit_bytes=4 * 1024 * 1024),
+    )(*[pltpu.with_memory_space_constraint(one, pltpu.VMEM) for one in made])
     video_out, gvq, gvk, gvv, audio_out, gaq, gak, gav = wrote
     return video_out, audio_out, gvq, gvk, gvv, gaq, gak, gav
 

time: 88.8 us -> 81.9 us (0.922)
  local copies, waits for them, and re-layouts: 4.2 us -> 0 us
  Pallas kernels: 83.7 us -> 80.9 us
    unnamed x10 -> x0, local copies, waits for them, and re-layouts: 4.2 us -> none
    pallas_call x1, Pallas kernels: 4.24 us -> 2.4 us  [shards(): pl.pallas_call(write_kernel, out_shape=(big,) * 4 + (small,) * 4, in_spec...]
    pallas_call x1, Pallas kernels: 79.4 us -> 78.5 us  [shards(): pl.pallas_call(kernel, out_shape=(vmem((ROWS, LOCAL), BF16),) * 4 + (vmem...]
where the time goes in v6:
time: 81.9 us; the launch traced here: 81.7 us
  Pallas kernels  80.9 us (99%)
    pallas_call x1, Pallas kernels, shards(): pl.pallas_call(kernel, out_shape=(vmem((ROWS, LOCAL), BF16),) * 4 + (vmem...  78.5 us
    pallas_call x1, Pallas kernels, shards(): pl.pallas_call(write_kernel, out_shape=(big,) * 4 + (small,) * 4, in_spec...  2.4 us

profile of v6, /device:TPU:1, one launch (start us, length us, event | category | flops | bytes accessed | tf_op | source)
XLA Modules:
  0.0 81.7 jit_solution(15045877967047157190)
XLA Ops:
  0.6 78.5 %shard_map.179 = (bf16[512,768]{1,0:T(8,128)(2,1)S(1)}, bf16[512,768]{1,0:T(8,128)(2,1)S(1)}, bf16[512,768]{1,0:T(8,128)(2,1)S(1)}, bf16[512,768]{1,0:T(8,128)(2,1)S(1)}, f32[4,8,768]{2,1,0:T(8,128)S(1)}) custom-call(bf16[512,768]{1,0:T(8,128)(2,1)} %vq_in.1, bf16[512,768]{1,0:T(8,128)(2,1)} %vk_in.1, bf16[512,768]{1,0:T(8,128)(2,1)} %vv_in.1, ...), custom_call_target="tpu_custom_call" | custom-call | tf_op jit(solution)/shard_map/pallas_call | solution.py:649
  79.2 2.4 %shard_map.180 = (bf16[512,768]{1,0:T(8,128)(2,1)}, bf16[512,768]{1,0:T(8,128)(2,1)}, bf16[512,768]{1,0:T(8,128)(2,1)}, bf16[512,768]{1,0:T(8,128)(2,1)}, bf16[8...) custom-call(bf16[512,768]{1,0:T(8,128)(2,1)S(1)} %get-tuple-element.21.a, ...), custom_call_target="tpu_custom_call" | custom-call | tf_op jit(solution)/shard_map/pallas_call | solution.py:660

commit v7 on v6

--- a/solution.py
+++ b/solution.py
@@ -144,11 +144,7 @@
         high = jnp.where(c == 0, other, mine)
         return jnp.concatenate([low, high], axis=0)
 
-    def ag_p(ch, copies):
-        done(copies)
-        for a in range(2):
-            G[c, ch, q, p, zh, a] = chip_rows(PK[ch, 0], PR[ch, 0], a).astype(BF16)
-            G[c, ch, q, p, 1 - zh, a] = chip_rows(PR[ch, 1], PR[ch, 2], a).astype(BF16)
+    def ag_p(ch):
         block = G.at[c, ch, q, p]
         return go(*[copy(block, block, to) for to in ring_p])
 
@@ -170,42 +166,57 @@
         return go(copy(one, one, right_q), copy(two, two, left_q))
 
     pack(0, (av, ado))
+    pack(1, (aq, ak))
+    sender = 4 * hd + 2 * zh + c
     for i, raw in enumerate((aq, ak)):
         block = raw[...].astype(F32)
         total = jnp.sum(block * block, axis=1, keepdims=True)
-        HSA[hd, i] = jnp.broadcast_to(total, (8, D))
+        HSA[sender, i] = jnp.broadcast_to(total, (8, D))
     pl.semaphore_wait(barrier, len(partners))
-    sums_a = go(*[copy(HSA.at[hd], HSA.at[hd], to) for to in heads])
     first0 = ag_first(0)
-    pack(2, (aq, ak))
-    raws = ag_first(2)
+    first1 = ag_first(1)
+    mine = HSA.at[sender]
+    first1 += go(*[copy(mine, mine, to) for to in near + heads + far[0] + far[1] + far[2]])
 
     HS[hd] = jnp.zeros((8, 512), F32)
-
-    def video_sum(i, raw):
+    for i, raw in enumerate((vq, vk)):
         loads[i].wait()
         total = jnp.zeros((ROWS, D), F32)
         for b in range(NH):
             block = raw[:, b * D : (b + 1) * D].astype(F32)
             total = total + block * block
         HS[hd, i : i + 1, :] = row_of(total)
-
-    video_sum(0, vq)
-    done(sums_a)
-    inv_a = []
-    for i, (raw, gain) in enumerate(((aq, gaq_gain), (ak, gak_gain))):
-        total = HSA[0, i] + HSA[1, i] + HSA[2, i] + HSA[3, i]
-        inv_a.append(lax.rsqrt(total / WIDTH + EPS))
-        wide = jnp.concatenate([inv_a[i]] * NH, axis=1)
-        sm[i] = (raw[...].astype(F32) * wide * gain[...]).astype(BF16).astype(F32)
-    pack(1, (sm.at[0], sm.at[1]))
-    first1 = ag_first(1)
-    ring0 = ag_p(0, first0)
-    video_sum(1, vk)
     sums = go(*[copy(HS.at[hd], HS.at[hd], to) for to in heads])
-    ring1 = ag_p(1, first1)
-    q10 = ag_q1(0, ring0)
-    go(forward(0, 0))
+
+    done(first0)
+    for a in range(2):
+        G[c, 0, q, p, zh, a] = chip_rows(PK[0, 0], PR[0, 0], a).astype(BF16)
+        G[c, 0, q, p, 1 - zh, a] = chip_rows(PR[0, 1], PR[0, 2], a).astype(BF16)
+    ring0 = ag_p(0)
+
+    done(first1)
+
+    def inverse(zz, cc, i):
+        total = HSA[2 * zz + cc, i]
+        for k in range(1, 4):
+            total = total + HSA[4 * k + 2 * zz + cc, i]
+        return lax.rsqrt(total / WIDTH + EPS)
+
+    for i, gain in enumerate((gaq_gain, gak_gain)):
+        raws = chip_rows(PK[1, 0], PR[1, 0], i), chip_rows(PR[1, 1], PR[1, 2], i)
+        for zz, raw in zip((zh, 1 - zh), raws):
+            inv_row = jnp.concatenate([inverse(zz, cc, i) for cc in range(2)], axis=0)
+            wide = jnp.concatenate([inv_row] * 3, axis=1)
+            half = gain[:, half_of[0]]
+            G[c, 1, q, p, zz, i] = (raw * wide * half).astype(BF16)
+            RA[zz, i] = raw * half
+    ring1 = ag_p(1)
+    inv_a = [inverse(zh, c, i) for i in range(2)]
+
+    loads[2].wait()
+    for b in range(NH):
+        at_b = slice(b * D, (b + 1) * D)
+        vvT[at_b, :] = jnp.transpose(vv[:, at_b])
     done(sums)
     total = HS[0] + HS[1] + HS[2] + HS[3]
     inv = lax.rsqrt(total / WIDTH + EPS)
@@ -217,9 +228,11 @@
             out[:, at_b] = (raw[:, at_b].astype(F32) * inv_col[i] * gain[:, at_b]).astype(BF16)
 
     norm_video(1, vk, gvk_gain, vkn)
+    q10 = ag_q1(0, ring0)
+    go(forward(0, 0))
+    norm_video(0, vq, gvq_gain, vqn)
     q11 = ag_q1(1, ring1)
     go(forward(1, 0))
-    norm_video(0, vq, gvq_gain, vqn)
     for b in range(NH):
         at_b = slice(b * D, (b + 1) * D)
         vkT[at_b, :] = jnp.transpose(vkn[:, at_b])
@@ -297,10 +310,6 @@
 
         lax.fori_loop(0, 2, step, 0)
 
-    loads[2].wait()
-    for b in range(NH):
-        at_b = slice(b * D, (b + 1) * D)
-        vvT[at_b, :] = jnp.transpose(vv[:, at_b])
     audio(c, q)
     loads[3].wait()
     video(c, q)
@@ -340,10 +349,6 @@
     level0 = stats_start(0, (sib, opp, opp_sib))
     video(c, q2)
     twice(lambda n: video(o, *pair(n)))
-    done(raws)
-    for i, gain in enumerate((gaq_gain, gak_gain)):
-        RA[zh, i] = chip_rows(PK[2, 0], PR[2, 0], i) * gain[:, half_of[0]]
-        RA[1 - zh, i] = chip_rows(PR[2, 1], PR[2, 2], i) * gain[:, half_of[0]]
 
     IA[...] = jnp.zeros_like(IA)
     base_cross = slots(6)
@@ -410,7 +415,6 @@
         rows = go(
             *[copy(TZ.at[ch, zz, cc], RB4.at[ch, k], near[k]) for k, (zz, cc) in enumerate(place[1:])]
         )
-        sender = 4 * hd + 2 * zh + c
         slot = HAr.at[ch, sender]
         HAr[ch, sender] = HAs[ch, zh, c]
         targets = [(place[0], to) for to in heads]
@@ -606,9 +610,9 @@
         vmem((8, LOCAL), F32),
         vmem((2, 2, 16, HALF), F32),
         vmem((2, 2, 4, 4, 2, 2, 16, HALF), BF16),
-        vmem((3, 2, 16, HALF), BF16),
-        vmem((3, 3, 16, HALF), BF16),
-        vmem((4, 2, 8, D), F32),
+        vmem((2, 2, 16, HALF), BF16),
+        vmem((2, 3, 16, HALF), BF16),
+        vmem((16, 2, 8, D), F32),
         vmem((4, 8, 512), F32),
         vmem((2, 4, 8, 512), F32),
         vmem((2, 2, 2, 8, D), F32),

time: 81.9 us -> 81.3 us (level)
  no operation moved by 1% of the time
where the time goes in v7:
time: 81.3 us; the launch traced here: 81.1 us
  Pallas kernels  80.3 us (99%)
    pallas_call x1, Pallas kernels, shards(): pl.pallas_call(kernel, out_shape=(vmem((ROWS, LOCAL), BF16),) * 4 + (vmem...  77.9 us
    pallas_call x1, Pallas kernels, shards(): pl.pallas_call(write_kernel, out_shape=(big,) * 4 + (small,) * 4, in_spec...  2.4 us

profile of v7, /device:TPU:1, one launch (start us, length us, event | category | flops | bytes accessed | tf_op | source)
XLA Modules:
  0.0 81.1 jit_solution(16279724287624457593)
XLA Ops:
  0.6 77.9 %shard_map.179 = (bf16[512,768]{1,0:T(8,128)(2,1)S(1)}, bf16[512,768]{1,0:T(8,128)(2,1)S(1)}, bf16[512,768]{1,0:T(8,128)(2,1)S(1)}, bf16[512,768]{1,0:T(8,128)(2,1)S(1)}, f32[4,8,768]{2,1,0:T(8,128)S(1)}) custom-call(bf16[512,768]{1,0:T(8,128)(2,1)} %vq_in.1, bf16[512,768]{1,0:T(8,128)(2,1)} %vk_in.1, bf16[512,768]{1,0:T(8,128)(2,1)} %vv_in.1, ...), custom_call_target="tpu_custom_call" | custom-call | tf_op jit(solution)/shard_map/pallas_call | solution.py:653
  78.6 2.4 %shard_map.180 = (bf16[512,768]{1,0:T(8,128)(2,1)}, bf16[512,768]{1,0:T(8,128)(2,1)}, bf16[512,768]{1,0:T(8,128)(2,1)}, bf16[512,768]{1,0:T(8,128)(2,1)}, bf16[8...) custom-call(bf16[512,768]{1,0:T(8,128)(2,1)S(1)} %get-tuple-element.21.a, ...), custom_call_target="tpu_custom_call" | custom-call | tf_op jit(solution)/shard_map/pallas_call | solution.py:664

commit v8 on v7

--- a/solution.py
+++ b/solution.py
@@ -51,7 +51,7 @@
     vq_in, vk_in, vv_in, vdo_in, aq, ak, av, ado, gain0, gain1, gain2, gain3,
     video_out, out_gvq, out_gvk, out_gvv, out_small,
     vq, vk, vv, vdo, GN, RA,
-    G, PK, PR, HSA, HS, HI, HAs, HAr, vqn, vkn, vvT, vkT, inv_col, E, DP, EV, DV, SV, ST, SR, WT,
+    G, PK, PR, HSA, HS, HI, HAs, HAr, vqn, vkn, inv_col, E, DP, EV, DV, SV, ST, SR, WT,
     GQ, GK, IA, Xs, Xr, R, RB1, RB2, S, RB3, TF, TZ, RB4, sm,
     send, recv, local,
 ):
@@ -214,9 +214,6 @@
     inv_a = [inverse(zh, c, i) for i in range(2)]
 
     loads[2].wait()
-    for b in range(NH):
-        at_b = slice(b * D, (b + 1) * D)
-        vvT[at_b, :] = jnp.transpose(vv[:, at_b])
     done(sums)
     total = HS[0] + HS[1] + HS[2] + HS[3]
     inv = lax.rsqrt(total / WIDTH + EPS)
@@ -233,9 +230,6 @@
     norm_video(0, vq, gvq_gain, vqn)
     q11 = ag_q1(1, ring1)
     go(forward(1, 0))
-    for b in range(NH):
-        at_b = slice(b * D, (b + 1) * D)
-        vkT[at_b, :] = jnp.transpose(vkn[:, at_b])
 
     def lanes_of(i):
         return pl.ds(pl.multiple_of(i * D, D), D)
@@ -410,17 +404,19 @@
                 TF[ch, zz, cc] = tile
                 TZ[ch, zz, cc] = tile.astype(BF16)
             inner = jnp.sum(RA[zz, 1 - ch] * both[ch], axis=1, keepdims=True)
-            HAs[ch, zz] = jnp.broadcast_to(inner, (16, D)).reshape(2, 8, D)
+            HAs[zz, :, ch] = jnp.broadcast_to(inner, (16, D)).reshape(2, 8, D)
         place = ((zh, c), (zh, o), (1 - zh, c), (1 - zh, o))
         rows = go(
             *[copy(TZ.at[ch, zz, cc], RB4.at[ch, k], near[k]) for k, (zz, cc) in enumerate(place[1:])]
         )
-        slot = HAr.at[ch, sender]
-        HAr[ch, sender] = HAs[ch, zh, c]
+        if ch == 0:
+            return rows
+        slot = HAr.at[sender]
+        HAr[sender] = HAs[zh, c]
         targets = [(place[0], to) for to in heads]
         for k in range(3):
             targets += [(place[k + 1], to) for to in [near[k]] + far[k]]
-        return rows + go(*[copy(HAs.at[ch, zz, cc], slot, to) for (zz, cc), to in targets])
+        return rows + go(*[copy(HAs.at[zz, cc], slot, to) for (zz, cc), to in targets])
 
     def rs_end(ch, copies, slots):
         done(copies)
@@ -460,12 +456,11 @@
             chunk, lanes = slice(256 * t, 256 * (t + 1)), lanes_of(3 * h + j)
             grads = dot(ds, vqn[chunk, lanes], NN), dot(low, vdo[chunk, lanes], NN)
             if t == 0:
-                keys = jnp.transpose(some_rows(1, h, range(4), 1, j))
-                values = jnp.transpose(some_rows(0, h, range(4), 0, j))
+                keys, values = some_rows(1, h, range(4), 1, j), some_rows(0, h, range(4), 0, j)
                 sums[j] = grads + (keys, values)
             keys, values = sums[j][2:]
-            video_out[chunk, lanes] = jnp.transpose(dot(values, low, NN)).astype(BF16)
-            grad_q = jnp.transpose(dot(keys, ds, NN)) * FACTOR
+            video_out[chunk, lanes] = dot(low, values, TN).astype(BF16)
+            grad_q = dot(ds, keys, TN) * FACTOR
             GQ[chunk, lanes] = grad_q
             IA[0, chunk] += vq[chunk, lanes].astype(F32) * gvq_gain[:, lanes] * grad_q
             if t == 0:
@@ -526,8 +521,8 @@
             low, ds = made
             lanes = lanes_of(3 * h + j)
             chunks = slice(2 * t, 2 * t + 2)
-            numer = jnp.transpose(dot(vvT[lanes, :], low, NN))
-            grad_q = jnp.transpose(dot(vkT[lanes, :], ds, NN)) * FACTOR
+            numer = dot(low, vv[:, lanes], TN)
+            grad_q = dot(ds, vkn[:, lanes], TN) * FACTOR
             if own and t == 0:
                 cross(1, j).wait()
             put(1, j, own, chunks, 0, numer)
@@ -576,9 +571,9 @@
     out_small[3] = sm[4]
     parts = ((aq, gaq_gain, sm[2]), (ak, gak_gain, sm[3]))
     for i, (raw, gain, grad) in enumerate(parts):
-        total = HAr[1 - i, 0]
+        total = HAr[0, 1 - i]
         for k in range(1, 16):
-            total = total + HAr[1 - i, k]
+            total = total + HAr[k, 1 - i]
         total = total / WIDTH
         wide = jnp.concatenate([inv_a[i]] * NH, axis=1)
         scale = jnp.concatenate([inv_a[i] * inv_a[i] * inv_a[i] * total] * NH, axis=1)
@@ -616,11 +611,9 @@
         vmem((4, 8, 512), F32),
         vmem((2, 4, 8, 512), F32),
         vmem((2, 2, 2, 8, D), F32),
-        vmem((2, 16, 8, D), F32),
+        vmem((16, 2, 8, D), F32),
         vmem((ROWS, LOCAL), BF16),
         vmem((ROWS, LOCAL), BF16),
-        vmem((LOCAL, ROWS), BF16),
-        vmem((LOCAL, ROWS), BF16),
         vmem((2, ROWS, D), F32),
         vmem((NH, ROWS, TOK), F32),
         vmem((NH, ROWS, TOK), F32),

time: 81.3 us -> 81.8 us (level)
  no operation moved by 1% of the time
where the time goes in v8:
time: 81.8 us; the launch traced here: 81.7 us
  Pallas kernels  80.9 us (99%)
    pallas_call x1, Pallas kernels, shards(): pl.pallas_call(kernel, out_shape=(vmem((ROWS, LOCAL), BF16),) * 4 + (vmem...  78.5 us
    pallas_call x1, Pallas kernels, shards(): pl.pallas_call(write_kernel, out_shape=(big,) * 4 + (small,) * 4, in_spec...  2.4 us

profile of v8, /device:TPU:1, one launch (start us, length us, event | category | flops | bytes accessed | tf_op | source)
XLA Modules:
  0.0 81.7 jit_solution(1468707633185760887)
XLA Ops:
  0.6 78.5 %shard_map.179 = (bf16[512,768]{1,0:T(8,128)(2,1)S(1)}, bf16[512,768]{1,0:T(8,128)(2,1)S(1)}, bf16[512,768]{1,0:T(8,128)(2,1)S(1)}, bf16[512,768]{1,0:T(8,128)(2,1)S(1)}, f32[4,8,768]{2,1,0:T(8,128)S(1)}) custom-call(bf16[512,768]{1,0:T(8,128)(2,1)} %vq_in.1, bf16[512,768]{1,0:T(8,128)(2,1)} %vk_in.1, bf16[512,768]{1,0:T(8,128)(2,1)} %vv_in.1, ...), custom_call_target="tpu_custom_call" | custom-call | tf_op jit(solution)/shard_map/pallas_call | solution.py:646
  79.1 2.4 %shard_map.180 = (bf16[512,768]{1,0:T(8,128)(2,1)}, bf16[512,768]{1,0:T(8,128)(2,1)}, bf16[512,768]{1,0:T(8,128)(2,1)}, bf16[512,768]{1,0:T(8,128)(2,1)}, bf16[8...) custom-call(bf16[512,768]{1,0:T(8,128)(2,1)S(1)} %get-tuple-element.21.a, ...), custom_call_target="tpu_custom_call" | custom-call | tf_op jit(solution)/shard_map/pallas_call | solution.py:657

commit v9 on v7

--- a/solution.py
+++ b/solution.py
@@ -82,16 +82,16 @@
     qn, qb, q2 = (q + 1) % 4, (q + 3) % 4, (q + 2) % 4
     right_q, left_q = ring_q[0], ring_q[2]
 
-    barrier = pltpu.get_barrier_semaphore()
-    partners = near + ring_p + ring_q + heads + far[0] + far[1] + far[2]
-    for partner in partners:
-        pl.semaphore_signal(barrier, inc=1, device_id=partner, device_id_type=MESH)
     loads = [
         pltpu.make_async_copy(src, dst, local.at[i])
         for i, (src, dst) in enumerate(((vq_in, vq), (vk_in, vk), (vv_in, vv), (vdo_in, vdo)))
     ]
     for one in loads:
         one.start()
+    barrier = pltpu.get_barrier_semaphore()
+    partners = near + ring_p + ring_q + heads + far[0] + far[1] + far[2]
+    for partner in partners:
+        pl.semaphore_signal(barrier, inc=1, device_id=partner, device_id_type=MESH)
     for i, gain in enumerate((gain0, gain1, gain2, gain3)):
         GN[i : i + 1, :] = gain[...].reshape(1, LOCAL)
     gvq_gain, gvk_gain, gaq_gain, gak_gain = (GN.at[i : i + 1] for i in range(4))
@@ -410,17 +410,19 @@
                 TF[ch, zz, cc] = tile
                 TZ[ch, zz, cc] = tile.astype(BF16)
             inner = jnp.sum(RA[zz, 1 - ch] * both[ch], axis=1, keepdims=True)
-            HAs[ch, zz] = jnp.broadcast_to(inner, (16, D)).reshape(2, 8, D)
+            HAs[zz, :, ch] = jnp.broadcast_to(inner, (16, D)).reshape(2, 8, D)
         place = ((zh, c), (zh, o), (1 - zh, c), (1 - zh, o))
         rows = go(
             *[copy(TZ.at[ch, zz, cc], RB4.at[ch, k], near[k]) for k, (zz, cc) in enumerate(place[1:])]
         )
-        slot = HAr.at[ch, sender]
-        HAr[ch, sender] = HAs[ch, zh, c]
+        if ch == 0:
+            return rows
+        slot = HAr.at[sender]
+        HAr[sender] = HAs[zh, c]
         targets = [(place[0], to) for to in heads]
         for k in range(3):
             targets += [(place[k + 1], to) for to in [near[k]] + far[k]]
-        return rows + go(*[copy(HAs.at[ch, zz, cc], slot, to) for (zz, cc), to in targets])
+        return rows + go(*[copy(HAs.at[zz, cc], slot, to) for (zz, cc), to in targets])
 
     def rs_end(ch, copies, slots):
         done(copies)
@@ -576,9 +578,9 @@
     out_small[3] = sm[4]
     parts = ((aq, gaq_gain, sm[2]), (ak, gak_gain, sm[3]))
     for i, (raw, gain, grad) in enumerate(parts):
-        total = HAr[1 - i, 0]
+        total = HAr[0, 1 - i]
         for k in range(1, 16):
-            total = total + HAr[1 - i, k]
+            total = total + HAr[k, 1 - i]
         total = total / WIDTH
         wide = jnp.concatenate([inv_a[i]] * NH, axis=1)
         scale = jnp.concatenate([inv_a[i] * inv_a[i] * inv_a[i] * total] * NH, axis=1)
@@ -588,12 +590,8 @@
 def write_kernel(
     a, b, c, d, small, out_a, out_b, out_c, out_d, small_0, small_1, small_2, small_3, sems
 ):
-    parts = ROWS // 4
-    copies = []
-    for i, (src, dst) in enumerate(((a, out_a), (b, out_b), (c, out_c), (d, out_d))):
-        for k in range(4):
-            rows = slice(k * parts, (k + 1) * parts)
-            copies.append(pltpu.make_async_copy(src.at[rows], dst.at[rows], sems.at[4 * i + k]))
+    pairs = ((a, out_a), (b, out_b), (c, out_c), (d, out_d))
+    copies = [pltpu.make_async_copy(src, dst, sems.at[i]) for i, (src, dst) in enumerate(pairs)]
     for one in copies:
         one.start()
     for i, out in enumerate((small_0, small_1, small_2, small_3)):
@@ -616,7 +614,7 @@
         vmem((4, 8, 512), F32),
         vmem((2, 4, 8, 512), F32),
         vmem((2, 2, 2, 8, D), F32),
-        vmem((2, 16, 8, D), F32),
+        vmem((16, 2, 8, D), F32),
         vmem((ROWS, LOCAL), BF16),
         vmem((ROWS, LOCAL), BF16),
         vmem((LOCAL, ROWS), BF16),
@@ -666,7 +664,7 @@
         out_shape=(big,) * 4 + (small,) * 4,
         in_specs=[spec] * 5,
         out_specs=(anywhere,) * 4 + (spec,) * 4,
-        scratch_shapes=[pltpu.SemaphoreType.DMA((16,))],
+        scratch_shapes=[pltpu.SemaphoreType.DMA((4,))],
         compiler_params=pltpu.CompilerParams(vmem_limit_bytes=4 * 1024 * 1024),
     )(*[pltpu.with_memory_space_constraint(one, pltpu.VMEM) for one in made])
     video_out, gvq, gvk, gvv, audio_out, gaq, gak, gav = wrote

time: 81.3 us -> 81.6 us (level)
  no operation moved by 1% of the time
where the time goes in v9:
time: 81.6 us; the launch traced here: 81.5 us
  Pallas kernels  80.7 us (99%)
    pallas_call x1, Pallas kernels, shards(): pl.pallas_call(kernel, out_shape=(vmem((ROWS, LOCAL), BF16),) * 4 + (vmem...  78.3 us
    pallas_call x1, Pallas kernels, shards(): pl.pallas_call(write_kernel, out_shape=(big,) * 4 + (small,) * 4, in_spec...  2.31 us

profile of v9, /device:TPU:1, one launch (start us, length us, event | category | flops | bytes accessed | tf_op | source)
XLA Modules:
  0.0 81.5 jit_solution(15525071256757619118)
XLA Ops:
  0.6 78.3 %shard_map.179 = (bf16[512,768]{1,0:T(8,128)(2,1)S(1)}, bf16[512,768]{1,0:T(8,128)(2,1)S(1)}, bf16[512,768]{1,0:T(8,128)(2,1)S(1)}, bf16[512,768]{1,0:T(8,128)(2,1)S(1)}, f32[4,8,768]{2,1,0:T(8,128)S(1)}) custom-call(bf16[512,768]{1,0:T(8,128)(2,1)} %vq_in.1, bf16[512,768]{1,0:T(8,128)(2,1)} %vk_in.1, bf16[512,768]{1,0:T(8,128)(2,1)} %vv_in.1, ...), custom_call_target="tpu_custom_call" | custom-call | tf_op jit(solution)/shard_map/pallas_call | solution.py:651
  79.0 2.3 %shard_map.180 = (bf16[512,768]{1,0:T(8,128)(2,1)}, bf16[512,768]{1,0:T(8,128)(2,1)}, bf16[512,768]{1,0:T(8,128)(2,1)}, bf16[512,768]{1,0:T(8,128)(2,1)}, bf16[8...) custom-call(bf16[512,768]{1,0:T(8,128)(2,1)S(1)} %get-tuple-element.21.a, ...), custom_call_target="tpu_custom_call" | custom-call | tf_op jit(solution)/shard_map/pallas_call | solution.py:662
